TPU v7x, 32 devices: a whole 2x2x4 slice. The times are simulated.
32 devices in a mesh: dp: 4 (over y, core), seq: 8 (over z, x).
Axes of the slice: x: 2, y: 2, z: 4, core: 2. Of those that a mesh axis runs over, the one named last changes fastest.
Arguments:
- features: bfloat16 [4, 6144, 512], P('dp', 'seq'), may hold values from -12 to 12, as said below
- slot_kind: int32 [4, 24], P('dp', 'seq'), may hold values from 0 to 2, as said below
- block_gain: float32 [512], replicated, may hold values from 0.1 to 1.9
- block_shift: float32 [512], replicated, may hold values from -2 to 2
- block_weight: bfloat16 [4608, 512], replicated, may hold values from -0.09375 to 0.09375
- block_bias: float32 [512], replicated, may hold values from -2 to 2
- final_gain: float32 [512], replicated, may hold values from 0.1 to 1.9
- final_shift: float32 [512], replicated, may hold values from -2 to 2
- latent_weight: bfloat16 [512, 144], replicated, may hold values from -0.09375 to 0.09375
- latent_bias: float32 [16], replicated, may hold values from -2 to 2
- embed_weight: bfloat16 [64, 1152], P(None, 'dp'), may hold values from -0.75 to 0.75
- embed_bias: bfloat16 [1152], P('dp'), may hold values from -2 to 2
Outputs:
- sequence: bfloat16 [4, 1024, 1152], P('dp', 'seq')
Inputs may be any that keep to these rules, and one draw needn't show every extreme that they name: `slot_kind`: the live slots of a device (kind 1 or 2) come before its empty ones. In every dp group, the live slots of the devices with seq index below d number between 2 d and 2 d + 2, and 2 * 8 over the whole group; in every group some device has 3 live slots. `features`: finite values.
All inputs are finite; a program needn't handle non-finite values.
Results may differ from a plain program's by a relative error of at most 0.014.
Values may be sent and summed in bfloat16 or wider, within the bound.
No kernel may reach another device: no remote copies, remote signals or barrier semaphores. Data moves between devices by JAX's collectives and lax.ppermute only.
A program may use at most 64 MiB of HBM per device.

v0:
```python
import jax
import jax.numpy as jnp
from jax import lax
from jax.sharding import PartitionSpec as P

GROUPS = 32
SLOT_ROWS = 32
SLOT_COLS = 8


LATENT_SHIFT = 0.0609
LATENT_SCALE = 1.5305
NORM_EPSILON = 1e-06
OFFSETS = [(-1, -1), (-1, 0), (-1, 1), (0, -1), (0, 0), (0, 1), (1, -1), (1, 0), (1, 1)]


def shifted(value, axis, steps):
    count = lax.axis_size(axis)
    leading, last = (max(0, -steps), min(count, count - steps))
    return lax.ppermute(value, axis, [(source, source + steps) for source in range(leading, last)])


def group_norm(values, slot_types, norm_gain, norm_shift):
    slot_count, height, across, channels = values.shape
    grouped = values.reshape(slot_count, 2, height // 2, across, GROUPS, channels // GROUPS)
    joined = (slot_types == 2)[:, None, None, None, None, None]
    half_centre = jnp.mean(grouped, axis=(2, 3, 5), keepdims=True)
    centre = jnp.where(joined, jnp.mean(half_centre, axis=1, keepdims=True), half_centre)
    centred = grouped - centre
    half_spread = jnp.mean(centred * centred, axis=(2, 3, 5), keepdims=True)
    spread = jnp.where(joined, jnp.mean(half_spread, axis=1, keepdims=True), half_spread)
    normed = (centred * lax.rsqrt(spread + NORM_EPSILON)).reshape(values.shape)
    return normed * norm_gain + norm_shift


def boundary_mask(slot_types, height, row_step, out_type):
    row_index = jnp.arange(height)
    edge_row = height // 2 if row_step < 0 else height // 2 - 1
    crossing = (slot_types == 1)[:, None] & (row_index == edge_row)[None, :]
    return jnp.where(crossing, 0.0, 1.0).astype(out_type)[:, :, None, None]


def neighbour(padded, slot_types, row_step, col_step):
    height = padded.shape[1] - 2
    across = padded.shape[2] - 2
    window = padded[
        :, 1 + row_step : 1 + row_step + height, 1 + col_step : 1 + col_step + across, :
    ]
    if row_step != 0:
        window = window * boundary_mask(slot_types, height, row_step, window.dtype)
    return window


def encode(
    slots,
    slot_types,
    block_gain,
    block_shift,
    block_weight,
    block_bias,
    final_gain,
    final_shift,
    latent_weight,
    latent_bias,
):
    slot_count, height, across, channels = slots.shape
    lat_width = latent_weight.shape[1] // 9
    first_act = jax.nn.silu(
        group_norm(slots.astype(jnp.float32), slot_types, block_gain, block_shift)
    ).astype(jnp.bfloat16)
    padded = jnp.pad(first_act, ((0, 0), (1, 1), (1, 1), (0, 0)))
    columns = jnp.concatenate(
        [neighbour(padded, slot_types, row_step, col_step) for row_step, col_step in OFFSETS],
        axis=-1,
    )
    conv_out = (
        jnp.dot(columns.reshape(-1, 9 * channels), block_weight, preferred_element_type=jnp.float32)
        + block_bias
    )
    inner = (
        (slots.reshape(-1, channels).astype(jnp.float32) + conv_out)
        .astype(jnp.bfloat16)
        .reshape(slots.shape)
    )
    second_act = jax.nn.silu(
        group_norm(inner.astype(jnp.float32), slot_types, final_gain, final_shift)
    ).astype(jnp.bfloat16)
    tap_terms = jnp.dot(
        second_act.reshape(-1, channels), latent_weight, preferred_element_type=jnp.float32
    )
    tap_terms = tap_terms.reshape(slot_count, height, across, 9 * lat_width)
    padded_terms = jnp.pad(tap_terms, ((0, 0), (1, 1), (1, 1), (0, 0)))
    latent = jnp.zeros((slot_count, height, across, lat_width), jnp.float32) + latent_bias
    for tap_number, (row_step, col_step) in enumerate(OFFSETS):
        piece_terms = padded_terms[..., tap_number * lat_width : (tap_number + 1) * lat_width]
        latent = latent + neighbour(piece_terms, slot_types, row_step, col_step)
    scaled = (latent - LATENT_SHIFT) * LATENT_SCALE
    patches = scaled.reshape(slot_count, height // 2, 2, across // 2, 2, lat_width).transpose(
        0, 1, 3, 2, 4, 5
    )
    return patches.reshape(slot_count * (height // 2) * (across // 2), 4 * lat_width).astype(
        jnp.bfloat16
    )


def local(
    features,
    slot_kind,
    block_gain,
    block_shift,
    block_weight,
    block_bias,
    final_gain,
    final_shift,
    latent_weight,
    latent_bias,
    embed_weight,
    embed_bias,
):
    seq_devices = lax.axis_size("seq")
    position = lax.axis_index("seq")
    slot_total = slot_kind.shape[1]
    channels = features.shape[2]
    all_types = lax.all_gather(slot_kind[0], "seq", axis=0, tiled=True)
    live_slots = (all_types.reshape(seq_devices, slot_total) > 0).astype(jnp.int32)
    counts = jnp.sum(live_slots, axis=1)
    starts = jnp.cumsum(counts) - counts
    embed_full, bias_full = (
        lax.all_gather(embed_weight, "dp", axis=1, tiled=True),
        lax.all_gather(embed_bias, "dp", axis=0, tiled=True),
    )
    own_slots = features[0].reshape(slot_total, SLOT_ROWS, SLOT_COLS, channels)
    carry_in = starts[position] - 2 * position
    slot_number = jnp.arange(2, dtype=jnp.int32)
    hid_width = embed_full.shape[1]
    padded = jnp.concatenate([own_slots, jnp.zeros_like(own_slots[:1])], axis=0)
    arrived = shifted(lax.dynamic_slice_in_dim(padded, 2 - carry_in, 2, 0), "seq", 1)
    kept = jnp.take(own_slots, jnp.maximum(slot_number - carry_in, 0), axis=0)
    incoming = (slot_number < carry_in).reshape((2,) + (1,) * (own_slots.ndim - 1))
    work_slots = jnp.where(incoming, arrived, kept)
    global_slot = 2 * position + slot_number
    owner = jnp.sum((starts[None, :] <= global_slot[:, None]).astype(jnp.int32), axis=1) - 1
    work_types = all_types[owner * slot_total + global_slot - starts[owner]]
    patches = encode(
        work_slots,
        work_types,
        block_gain,
        block_shift,
        block_weight,
        block_bias,
        final_gain,
        final_shift,
        latent_weight,
        latent_bias,
    )
    result = (
        jnp.dot(patches, embed_full, preferred_element_type=jnp.float32)
        + bias_full.astype(jnp.float32)
    ).astype(jnp.bfloat16)
    return result.reshape(1, -1, hid_width)


def solution(mesh):
    in_specs = (
        P("dp", "seq", None),
        P("dp", "seq"),
        P(),
        P(),
        P(),
        P(),
        P(),
        P(),
        P(),
        P(),
        P(None, "dp"),
        P("dp"),
    )
    out_specs = P("dp", "seq", None)
    return jax.shard_map(local, mesh=mesh, in_specs=in_specs, out_specs=out_specs, check_vma=False)
```

profile of v0, /device:TPU:0, one launch (start us, length us, event | category | flops | bytes accessed | tf_op | source)
XLA Modules:
  0.0 69.1 jit_solution(11839659187832956254)
XLA Ops:
  0.0 1.3 %dynamic-slice = u32[1]{0:T(128)} dynamic-slice(u32[32]{0:T(128)} %constant.89, u32[]{:T(128)S(6)} %add.212), dynamic_slice_sizes={1} | dynamic-slice | bytes 12
  1.9 0.8 %bitcast_dynamic-update-slice_fusion = s32[24]{0:T(128)S(1)} fusion(s32[24]{0:T(128)S(1)} %broadcast.406, u32[]{:T(128)} %bitcast.1, s32[1,3]{1,0:T(1,128)} %param.13), kind=kLoop, calls=%fused_computation.97 | loop fusion | bytes 112
  2.7 13.1 %all-reduce.3 = s32[24]{0:T(128)S(1)} all-reduce(s32[24]{0:T(128)S(1)} %bitcast_dynamic-update-slice_fusion), channel_id=2, replica_groups=mesh['dp'=4,'seq'=8] {'seq'}, use_global_device_ids=true, to_apply=%add.3 | all-reduce | flops 24 | bytes 192 | tf_op jit(solution)/shard_map/all_gather | solution.py:124
  16.1 0.6 dynamic_slice.6
  17.4 1.0 %pad_dynamic-slice_fusion = bf16[2,32,8,512]{3,2,1,0:T(8,128)(2,1)S(1)} fusion(s32[]{:T(128)S(6)} %select_n.102, bf16[3,32,8,512]{3,2,1,0:T(8,128)(2,1)} %bitcast.79), kind=kLoop, calls=%fused_computation.33 | loop fusion | bytes 1310724 | tf_op jit(solution)/shard_map/dynamic_slice | solution.py:137
  18.4 3.5 %collective-permute-start = (bf16[2,32,8,512]{3,2,1,0:T(8,128)(2,1)S(1)}, bf16[2,32,8,512]{3,2,1,0:T(8,128)(2,1)S(1)}, u32[]{:S(2)}, u32[]{:S(2)}) collective-permute-start(bf16[2,32,8,512]{3,2,1,0:T(8,128)(2,1)S(1)} %pad_dynamic-slice_fusion), channel_id=1, source_target_pairs={{0,1},{1,2},{2,3},{3,4},{4,5},{5,6},{6,7},{8,9},{9,10},{10,11},{11... | collective-permute-start | bytes 1572872 | tf_op jit(solution)/shard_map/ppermute | solution.py:20
  22.0 1.7 %gather_fusion = bf16[2,32,8,512]{3,2,1,0:T(8,128)(2,1)S(1)} fusion(bf16[3,32,8,512]{3,2,1,0:T(8,128)(2,1)} %bitcast.80, s32[1024]{0:T(1024)S(1)} %pad_clamp_fusion.2), kind=kCustom, calls=%fused_computation | custom fusion | bytes 1048584 | tf_op jit(solution)/shard_map/jit(_take)/gather | solution.py:138
  23.9 0.6 gather_fusion.1
  24.6 0.6 gather_fusion.2
  25.2 1.2 %dynamic-slice.1 = u32[1]{0:T(128)} dynamic-slice(u32[32]{0:T(128)} %constant.94, u32[]{:T(128)S(6)} %add.212), dynamic_slice_sizes={1} | dynamic-slice | bytes 12
  27.1 0.9 %dynamic-update-slice.1 = bf16[1152]{0:T(1024)(128)(2,1)S(1)} dynamic-update-slice(bf16[1152]{0:T(1024)(128)(2,1)S(1)} %broadcast.407, bf16[288]{0:T(512)(128)(2,1)} %param.23, u32[]{:T(128)} %bitcast.23) | dynamic-update-slice | bytes 1156
  28.0 5.6 %all-reduce.4 = bf16[1152]{0:T(1024)(128)(2,1)S(1)} all-reduce(bf16[1152]{0:T(1024)(128)(2,1)S(1)} %dynamic-update-slice.1), channel_id=1, replica_groups=mesh['dp'=4,'seq'=8] {'dp'}, use_global_device_ids=true, to_apply=%add.4 | all-reduce | flops 1152 | bytes 4608
  33.6 5.8 %all-gather.1 = bf16[4,288,64]{1,2,0:T(8,128)(2,1)S(1)} all-gather(bf16[1,288,64]{1,2,0:T(8,128)(2,1)} %bitcast.85), channel_id=1, replica_groups=mesh['dp'=4,'seq'=8] {'dp'}, dimensions={0}, use_global_device_ids=true | all-gather | bytes 184320 | tf_op jit(solution)/shard_map/all_gather | solution.py:129
  39.9 0.6 convert_reduce_fusion
  41.4 0.6 sub.90
  43.2 0.6 mul.165
  46.0 4.8 %fusion.5 = f32[512,512]{1,0:T(8,128)S(1)} fusion(bf16[2,32,8,512]{3,2,1,0:T(8,128)(2,1)S(1)} %get-tuple-element.6, f32[512]{0:T(512)S(1)} %copy-done.6, bf16[512,4608]{1,0:T(8,128)(2,1)S(1)} %bitcast.84, bf16[4608,512]{1,0:T(8,128)(2,1)} %param.16), kind=kOutput, calls=%fused_computation.35 | convolution fusion | flops 2417229824 | bytes 11012096 | tf_op jit(solution)/shard_map/dot_general | solution.py:77
  50.8 4.9 %reshape.348 = f32[2,2,16,8,32,16]{5,4,3,2,1,0:T(8,128)} reshape(f32[512,512]{1,0:T(8,128)S(1)} %fusion.5) | data formatting | bytes 2097152 | tf_op jit(solution)/shard_map/convert_element_type | solution.py:86
  55.7 4.3 %reduce_sum.114 = f32[2,2,32]{2,1,0:T(2,128)S(1)} reduce(f32[2,2,16,8,32,16]{5,4,3,2,1,0:T(8,128)} %reshape.348, f32[]{:T(128)} %constant.69.clone.1), dimensions={2,3,5}, to_apply=%region_9.10 | reduce | flops 262016 | bytes 1049092 | tf_op jit(solution)/shard_map/reduce_sum | solution.py:27
  60.1 4.7 %multiply_reduce_fusion = f32[2,2,32]{2,1,0:T(2,128)S(1)} fusion(f32[2,2,16,8,32,16]{5,4,3,2,1,0:T(8,128)} %reshape.348, f32[2,2,32]{2,1,0:T(2,128)S(1)} %broadcast_select_fusion), kind=kLoop, calls=%fused_computation.3 | loop fusion | flops 786304 | bytes 1049600 | tf_op jit(solution)/shard_map/reduce_sum | solution.py:30
  65.1 0.6 mul.181
  65.9 0.6 sub.94
  67.2 0.7 fusion.37
  68.1 0.9 %fusion.1 = bf16[1,128,1152]{2,1,0:T(8,128)(2,1)} fusion(bf16[128,64]{1,0:T(8,128)(2,1)S(1)} %convert_element_type.96, bf16[1152,64]{0,1:T(8,128)(2,1)S(1)} %reshape.381, f32[1152]{0:T(1024)S(1)} %convert_element_type.97), kind=kOutput, calls=%fused_computation.14 | convolution fusion | flops 19169280 | bytes 463360 | tf_op jit(solution)/shard_map/dot_general | solution.py:157
  (72 shorter events, 6.6 us)
Async XLA Ops:
  0.0 66.9 %copy-start = (bf16[512,144]{0,1:T(8,128)(2,1)S(1)}, bf16[512,144]{0,1:T(8,128)(2,1)}, u32[]{:S(2)}) copy-start(bf16[512,144]{0,1:T(8,128)(2,1)} %param.20) | copy-start | bytes 442372
  18.4 21.5 %collective-permute-start = (bf16[2,32,8,512]{3,2,1,0:T(8,128)(2,1)S(1)}, bf16[2,32,8,512]{3,2,1,0:T(8,128)(2,1)S(1)}, u32[]{:S(2)}, u32[]{:S(2)}) collective-permute-start(bf16[2,32,8,512]{3,2,1,0:T(8,128)(2,1)S(1)} %pad_dynamic-slice_fusion), channel_id=1, source_target_pairs={{0,1},{1,2},{2,3},{3,4},{4,5},{5,6},{6,7},{8,9},{9,10},{10,11},{11... | collective-permute-start | bytes 1572872 | tf_op jit(solution)/shard_map/ppermute | solution.py:20
  40.5 3.3 %copy-start.1 = (f32[512]{0:T(512)S(1)}, f32[512]{0:T(512)}, u32[]{:S(2)}) copy-start(f32[512]{0:T(512)} %param.15) | copy-start | bytes 6148
  40.5 3.3 %copy-start.2 = (f32[512]{0:T(512)S(1)}, f32[512]{0:T(512)}, u32[]{:S(2)}) copy-start(f32[512]{0:T(512)} %param.14) | copy-start | bytes 6148
  44.2 1.8 %copy-start.6 = (f32[512]{0:T(512)S(1)}, f32[512]{0:T(512)}, u32[]{:S(2)}) copy-start(f32[512]{0:T(512)} %param.17) | copy-start | bytes 6148
  60.1 6.5 %copy-start.3 = (f32[512]{0:T(512)S(1)}, f32[512]{0:T(512)}, u32[]{:S(2)}) copy-start(f32[512]{0:T(512)} %param.19) | copy-start | bytes 6148
  60.1 6.5 %copy-start.4 = (f32[512]{0:T(512)S(1)}, f32[512]{0:T(512)}, u32[]{:S(2)}) copy-start(f32[512]{0:T(512)} %param.18) | copy-start | bytes 6148
  64.8 2.4 %copy-start.5 = (f32[16]{0:T(128)S(1)}, f32[16]{0:T(128)}, u32[]{:S(2)}) copy-start(f32[16]{0:T(128)} %param.21) | copy-start | bytes 196
where the time goes:
time: 69.4 us; the launch traced here: 69.1 us
  blocking collectives  24.5 us (35%)
  local copies, waits for them, and re-layouts  18.5 us (27%)
  other arithmetic  14.1 us (20%)
  matrix products  6.03 us (9%)
  starting transfers between devices  3.53 us (5%)
  between operations  2.34 us (3%)
    all_gather x1, blocking collectives, local(): all_types = lax.all_gather(slot_kind[0], 'seq', axis=0, tiled=True)  13.1 us
    all_gather x1, blocking collectives, local(): lax.all_gather(embed_weight, 'dp', axis=1, tiled=True)  5.84 us
    unnamed x1, blocking collectives  5.64 us
    reduce_sum x3, other arithmetic, group_norm(): half_spread = jnp.mean(centred * centred, axis=(2, 3, 5), keepdims=True)  5.21 us
    reduce_sum x3, other arithmetic, group_norm(): half_centre = jnp.mean(grouped, axis=(2, 3, 5), keepdims=True)  5 us
    convert_element_type x1, local copies, waits for them, and re-layouts, encode(): inner.astype(jnp.float32)  4.89 us
    dot_general x1, matrix products, encode(): jnp.dot(columns.reshape(-1, 9 * channels), block_weight, preferred_elemen...  4.79 us
    unnamed x23, local copies, waits for them, and re-layouts  4.6 us
  transfers between devices with their start and end apart: 1, of which 0 were waited for; matrix products, arithmetic and copies ran while one was open for 8% of the time, Pallas kernels for 0%

commit v1 on v0

v1 whole, which is shorter than its diff:
```python
import functools
import jax
import jax.numpy as jnp
from jax import lax
from jax.sharding import PartitionSpec as P
from jax.experimental import pallas as pl
from jax.experimental.pallas import tpu as pltpu

GROUPS = 32
SLOT_ROWS = 32
SLOT_COLS = 8
LATENT_SHIFT = 0.0609
LATENT_SCALE = 1.5305
NORM_EPSILON = 1e-06
LANES = 128
VMEM_BYTES = 64 * 1024 * 1024
F32 = jnp.float32
BF16 = jnp.bfloat16


def group_total(stats, same_group):
    rows, channels = stats.shape
    chunks = channels // LANES
    packed = jnp.concatenate([stats[:, k * LANES:(k + 1) * LANES] for k in range(chunks)], axis=0)
    high = packed.astype(BF16)
    rest = packed - high.astype(F32)
    middle = rest.astype(BF16)
    low = (rest - middle.astype(F32)).astype(BF16)
    total = sum(jnp.dot(piece, same_group, preferred_element_type=F32) for piece in (high, middle, low))
    return jnp.concatenate([total[k * rows:(k + 1) * rows] for k in range(chunks)], axis=1)


def affine(stats, joined, gain, shift, same_group, count):
    total = group_total(stats, same_group)
    mean, square = total[0:2] * (1.0 / count), total[2:4] * (1.0 / count)
    both_mean = 0.5 * (mean[0:1] + mean[1:2])
    both_square = 0.5 * (square[0:1] + square[1:2])
    mean = jnp.where(joined, both_mean, mean)
    square = jnp.where(joined, both_square, square)
    spread = jnp.maximum(square - mean * mean, 0.0)
    scale = lax.rsqrt(spread + NORM_EPSILON) * (0.5 * gain)
    return scale, 0.5 * shift - mean * scale


def half_stats(half):
    total = jnp.sum(half, axis=0, keepdims=True)
    return total, jnp.sum(half * half, axis=0, keepdims=True)


def encode_slot(x_ref, joined, tables, prm, wbuf, wait_weights, lw_ref, z_ref, u_ref, y_ref):
    gain1, shift1, bias1, gain2, shift2, bias2 = prm
    same_group, perm, col_left, col_right, lane_b, lane_a = tables
    cells, channels = x_ref.shape
    half = cells // 2
    rows = cells // SLOT_COLS
    chunks = channels // LANES
    count = half * (channels // GROUPS)
    keep = jnp.where(joined, 1.0, 0.0).astype(F32)

    parts = []
    for k in range(chunks):
        x = x_ref[:, k * LANES:(k + 1) * LANES].astype(F32)
        t0, q0 = half_stats(x[:half])
        t1, q1 = half_stats(x[half:])
        parts.append(jnp.concatenate([t0, t1, q0, q1], axis=0))
    scale, offset = affine(jnp.concatenate(parts, axis=1), joined, gain1, shift1, same_group, count)
    zero = jnp.zeros((SLOT_COLS, LANES), F32)
    for k in range(chunks):
        lanes = slice(k * LANES, (k + 1) * LANES)
        x = x_ref[:, lanes].astype(F32)
        v = jnp.concatenate([x[:half] * scale[0:1, lanes] + offset[0:1, lanes],
                             x[half:] * scale[1:2, lanes] + offset[1:2, lanes]], axis=0)
        act = v + v * jnp.tanh(v)
        act3 = act.reshape(rows, SLOT_COLS, LANES)
        left = jnp.where(col_left, 0.0, pltpu.roll(act3, 1, 1)).reshape(cells, LANES)
        right = jnp.where(col_right, 0.0, pltpu.roll(act3, SLOT_COLS - 1, 1)).reshape(cells, LANES)
        for b, value in enumerate((left, act, right)):
            z_ref[b, :, lanes] = value.astype(BF16)
            over = value[half:half + SLOT_COLS] * keep
            under = value[half - SLOT_COLS:half] * keep
            u_ref[b, 0, :, lanes] = jnp.concatenate([zero, value[:half], over], axis=0).astype(BF16)
            u_ref[b, 1, :, lanes] = jnp.concatenate([under, value[half:], zero], axis=0).astype(BF16)

    conv = None
    for step, a in enumerate((0, -1, 1)):
        if a == 0:
            lhs = jnp.concatenate([z_ref[b] for b in range(3)], axis=1)
        else:
            first = 0 if a < 0 else 2 * SLOT_COLS
            lhs = jnp.concatenate(
                [jnp.concatenate([u_ref[b, h, first:first + half, :] for h in range(2)], axis=0) for b in range(3)],
                axis=1)
        wait_weights(step)
        depth = 3 * channels
        base = (a + 1) * depth
        term = jnp.dot(lhs, wbuf[base:base + depth, :], preferred_element_type=F32)
        conv = term if conv is None else conv + term

    parts = []
    for k in range(chunks):
        lanes = slice(k * LANES, (k + 1) * LANES)
        inner = (x_ref[:, lanes].astype(F32) + (conv[:, lanes] + bias1[0:1, lanes])).astype(BF16)
        y_ref[:, lanes] = inner
        inner = inner.astype(F32)
        t0, q0 = half_stats(inner[:half])
        t1, q1 = half_stats(inner[half:])
        parts.append(jnp.concatenate([t0, t1, q0, q1], axis=0))
    scale, offset = affine(jnp.concatenate(parts, axis=1), joined, gain2, shift2, same_group, count)
    for k in range(chunks):
        lanes = slice(k * LANES, (k + 1) * LANES)
        y = y_ref[:, lanes].astype(F32)
        v = jnp.concatenate([y[:half] * scale[0:1, lanes] + offset[0:1, lanes],
                             y[half:] * scale[1:2, lanes] + offset[1:2, lanes]], axis=0)
        y_ref[:, lanes] = (v + v * jnp.tanh(v)).astype(BF16)

    lat = lw_ref.shape[0] // 9
    taps = lax.dot_general(y_ref[...], lw_ref[...], (((1,), (1,)), ((), ())), preferred_element_type=F32)
    taps = jnp.concatenate([taps, jnp.zeros((cells, 2 * LANES - 9 * lat), F32)], axis=1).reshape(rows, SLOT_COLS, 2 * LANES)
    from_left = jnp.where(col_left, 0.0, pltpu.roll(taps, 1, 1))
    from_right = jnp.where(col_right, 0.0, pltpu.roll(taps, SLOT_COLS - 1, 1))
    moved = jnp.where(lane_b == 0, from_left, jnp.where(lane_b == 1, taps, from_right))
    blank = jnp.zeros((1, SLOT_COLS, 2 * LANES), F32)
    mid = rows // 2
    above = jnp.concatenate([blank, moved[:mid - 1], moved[mid - 1:mid] * keep, moved[mid:rows - 1]], axis=0)
    below = jnp.concatenate([moved[1:mid], moved[mid:mid + 1] * keep, moved[mid + 1:], blank], axis=0)
    moved = jnp.where(lane_a == 0, above, jnp.where(lane_a == 1, moved, below)).reshape(cells, 2 * LANES)
    folded = moved[:, :LANES]
    width = LANES // 2
    while width >= lat:
        folded = folded + pltpu.roll(folded, width, 1)
        width //= 2
    latent = (folded + moved[:, LANES:])[:, :lat]
    latent = ((latent + bias2) - LATENT_SHIFT) * LATENT_SCALE
    spread = jnp.dot(perm, latent.astype(BF16), preferred_element_type=F32)
    tokens = cells // 4
    return jnp.concatenate([spread[k * tokens:(k + 1) * tokens] for k in range(4)], axis=1).astype(BF16)


def make_tables(cells, channels, lat):
    width = channels // GROUPS
    r = lax.broadcasted_iota(jnp.int32, (LANES, LANES), 0) // width
    c = lax.broadcasted_iota(jnp.int32, (LANES, LANES), 1) // width
    same_group = jnp.where(r == c, 1.0, 0.0).astype(BF16)
    tokens = cells // 4
    half_cols = SLOT_COLS // 2
    row = lax.broadcasted_iota(jnp.int32, (cells, cells), 0)
    col = lax.broadcasted_iota(jnp.int32, (cells, cells), 1)
    block, token = row // tokens, row % tokens
    cell = (2 * (token // half_cols) + block // 2) * SLOT_COLS + 2 * (token % half_cols) + block % 2
    perm = jnp.where(cell == col, 1.0, 0.0).astype(BF16)
    sub = lax.broadcasted_iota(jnp.int32, (1, SLOT_COLS, 1), 1)
    lane = lax.broadcasted_iota(jnp.int32, (1, 1, 2 * LANES), 2)
    return same_group, perm, sub == 0, sub == SLOT_COLS - 1, (lane // lat) % 3, lane // (3 * lat)


def encode_kernel(ends, pack, kind_hbm, feat_ref, bw_ref, *rest):
    names = 7
    small_hbm, rest = rest[:names], rest[names:]
    if pack:
        ew_hbm, eb_hbm, out_ref, piece_ref, *rest = rest
    else:
        out_ref, *rest = rest
    kind_ref, xbuf, wbuf, z_ref, u_ref, y_ref, *rest = rest
    small, rest = rest[:names], rest[names:]
    if pack:
        ew_ref, eb_ref, *rest = rest
    ksem, xsem, wsem, ssem = rest
    slots = kind_ref.shape[1]
    cells, channels = xbuf.shape[1:]
    kcopy = pltpu.make_async_copy(kind_hbm, kind_ref, ksem)
    kcopy.start()
    xcopies = [pltpu.make_async_copy(feat_ref.at[0, pl.ds(s * cells, cells), :], xbuf.at[s], xsem.at[s])
               for s in range(slots)]
    depth = 3 * channels
    wcopies = [pltpu.make_async_copy(
        bw_ref.at[pl.ds((a + 1) * depth, depth), :], wbuf.at[pl.ds((a + 1) * depth, depth), :], wsem.at[i])
        for i, a in enumerate((0, -1, 1))]
    scopies = [pltpu.make_async_copy(src, dst, ssem.at[i]) for i, (src, dst) in enumerate(zip(small_hbm, small))]
    if pack:
        scopies += [pltpu.make_async_copy(ew_hbm, ew_ref, ssem.at[names]),
                    pltpu.make_async_copy(eb_hbm, eb_ref, ssem.at[names + 1])]
    for c in xcopies + scopies + wcopies:
        c.start()
    g1_ref, s1_ref, b1_ref, g2_ref, s2_ref, lw_ref, b2_ref = small
    lat = lw_ref.shape[0] // 9
    tables = make_tables(cells, channels, lat)
    kcopy.wait()
    live = jnp.int32(0)
    for s in range(slots):
        live = live + jnp.where(kind_ref[0, s] > 0, 1, 0).astype(jnp.int32)
    for c in scopies + xcopies:
        c.wait()
    row = lambda ref: ref[...].reshape(1, ref.shape[0])
    prm = (row(g1_ref), row(s1_ref), row(b1_ref), row(g2_ref), row(s2_ref), row(b2_ref))
    if pack:
        feats = ew_ref.shape[0]
        piece_ref[0:feats, :] = ew_ref[...]
        piece_ref[feats:, :] = jnp.broadcast_to(row(eb_ref), (piece_ref.shape[0] - feats, ew_ref.shape[1]))
    for k, end in enumerate(ends):
        slot = jnp.maximum(live - 1 - end, 0)
        wait = (lambda step: wcopies[step].wait()) if k == 0 else (lambda step: None)
        joined = kind_ref[0, slot] == 2
        out_ref[k] = encode_slot(xbuf.at[slot], joined, tables, prm, wbuf, wait, lw_ref, z_ref, u_ref, y_ref)


def encode(ends, features, slot_kind, block_gain, block_shift, block_weight, block_bias, final_gain, final_shift,
           latent_weight, latent_bias, embed=None):
    slots = slot_kind.shape[1]
    channels = features.shape[2]
    cells = SLOT_ROWS * SLOT_COLS
    lat = latent_weight.shape[1] // 9
    vmem = pl.BlockSpec(memory_space=pltpu.VMEM)
    hbm = pl.BlockSpec(memory_space=pltpu.HBM)
    n = len(ends)
    pack = embed is not None
    small = (block_gain, block_shift, block_bias, final_gain, final_shift, latent_weight.T, latent_bias)
    extra = tuple(embed) if pack else ()
    flops = n * cells * channels * 2 * (9 * channels + 9 * lat)
    outs = [jax.ShapeDtypeStruct((n, cells // 4, 4 * lat), BF16)]
    if pack:
        feats, width = embed[0].shape
        outs.append(jax.ShapeDtypeStruct((feats + 16, width), BF16))
    return pl.pallas_call(
        functools.partial(encode_kernel, ends, pack),
        out_shape=outs,
        in_specs=[hbm] * (3 + len(small) + len(extra)),
        out_specs=[vmem] * len(outs),
        scratch_shapes=[
            pltpu.SMEM(slot_kind.shape, jnp.int32),
            pltpu.VMEM((slots, cells, channels), BF16),
            pltpu.VMEM((9 * channels, channels), BF16),
            pltpu.VMEM((3, cells, channels), BF16),
            pltpu.VMEM((3, 2, cells // 2 + 2 * SLOT_COLS, channels), BF16),
            pltpu.VMEM((cells, channels), BF16),
        ] + [pltpu.VMEM(v.shape, v.dtype) for v in small + extra] + [
            pltpu.SemaphoreType.DMA,
            pltpu.SemaphoreType.DMA((slots,)),
            pltpu.SemaphoreType.DMA((3,)),
            pltpu.SemaphoreType.DMA((len(small + extra),)),
        ],
        compiler_params=pltpu.CompilerParams(vmem_limit_bytes=VMEM_BYTES),
        cost_estimate=pl.CostEstimate(flops=flops, bytes_accessed=9 * channels * channels * 2, transcendentals=0),
        name="encode_" + "_".join(map(str, ends)),
    )(slot_kind, features, block_weight, *small, *extra)


def join_kernel(parts, info_ref, own_ref, third_ref, even_ref, odd_ref, *rest):
    pieces, out_ref, embed_ref, source_ref = rest[:parts], *rest[parts:]
    carry, live, odd, group = (info_ref[k] for k in range(4))
    feats = pieces[0].shape[0] - 16
    width = pieces[0].shape[1]
    for j in range(parts):
        value = pieces[0][...]
        for k in range(1, parts):
            value = jnp.where((group ^ j) == k, pieces[k][...], value)
        embed_ref[:, j * width:(j + 1) * width] = value
    source_ref[0:2] = even_ref[...]
    source_ref[2:4] = odd_ref[...]
    source_ref[4:6] = own_ref[...]
    source_ref[6:7] = third_ref[...]
    tokens = own_ref.shape[1]
    weight = embed_ref[0:feats, :]
    bias = embed_ref[feats:feats + 1, :].astype(F32)
    for i in range(2):
        incoming = (1 - odd) * 2 + carry - 1 - i
        kept = 4 + live - 1 - (i - carry)
        patch = source_ref[jnp.clip(jnp.where(i < carry, incoming, kept), 0, 6)]
        value = jnp.dot(patch, weight, preferred_element_type=F32) + bias
        out_ref[0, i * tokens:(i + 1) * tokens, :] = value.astype(BF16)


def join(info, own, third, even, odd, pieces):
    parts = len(pieces)
    tall, width = pieces[0].shape
    vmem = pl.BlockSpec(memory_space=pltpu.VMEM)
    smem = pl.BlockSpec(memory_space=pltpu.SMEM)
    _, tokens, feats = own.shape
    return pl.pallas_call(
        functools.partial(join_kernel, parts),
        out_shape=jax.ShapeDtypeStruct((1, 2 * tokens, parts * width), BF16),
        in_specs=[smem] + [vmem] * (4 + parts),
        out_specs=vmem,
        scratch_shapes=[pltpu.VMEM((tall, parts * width), BF16), pltpu.VMEM((7, tokens, feats), BF16)],
        compiler_params=pltpu.CompilerParams(vmem_limit_bytes=8 * 1024 * 1024),
        cost_estimate=pl.CostEstimate(flops=4 * tokens * feats * parts * width, bytes_accessed=4 * tokens * parts * width,
                                      transcendentals=0),
        name="join",
    )(info, own, third, even, odd, *pieces)


def exchange(value, axis, offset):
    count = lax.axis_size(axis)
    return lax.ppermute(value, axis, [(i, i ^ offset) for i in range(count)])


def swap_odd_pairs(value, axis):
    count = lax.axis_size(axis)
    pairs = [(0, 0), (count - 1, count - 1)]
    for i in range(1, count - 1, 2):
        pairs += [(i, i + 1), (i + 1, i)]
    return lax.ppermute(value, axis, pairs)


def live_excess(kinds):
    return jnp.sum((kinds > 0).astype(jnp.int32)) - 2


def local(features, slot_kind, block_gain, block_shift, block_weight, block_bias, final_gain, final_shift,
          latent_weight, latent_bias, embed_weight, embed_bias):
    seq, dp = lax.axis_size("seq"), lax.axis_size("dp")
    position, group = lax.axis_index("seq"), lax.axis_index("dp")
    net = (features, slot_kind, block_gain, block_shift, block_weight, block_bias, final_gain, final_shift,
           latent_weight, latent_bias)
    excess = live_excess(slot_kind)
    below = jnp.int32(0)
    for offset in range(2, seq, 2):
        other = live_excess(exchange(slot_kind, "seq", offset))
        below = below + jnp.where((position ^ offset) < position, other, 0)
    own, piece = encode((0, 1), *net, embed=(embed_weight, embed_bias))
    sums = exchange(jnp.stack([below, below + excess]), "seq", 1)
    even = exchange(own, "seq", 1)
    odd = swap_odd_pairs(own, "seq")
    pieces = [piece] + [exchange(piece, "dp", offset) for offset in range(1, dp)]
    third, = encode((2,), *net)
    is_odd = position % 2
    carry = below + jnp.where(is_odd == 1, sums[1], sums[0])
    info = jnp.stack([carry, excess + 2, is_odd, group])
    return join(info, own, third, even, odd, pieces)


def solution(mesh):
    in_specs = (P("dp", "seq", None), P("dp", "seq")) + (P(),) * 8 + (P(None, "dp"), P("dp"))
    return jax.shard_map(local, mesh=mesh, in_specs=in_specs, out_specs=P("dp", "seq", None), check_vma=False)
```

time: 69.4 us -> 46.1 us (0.66)
  blocking collectives: 24.5 us -> 0 us
  Pallas kernels: 0 us -> 17.1 us
  local copies, waits for them, and re-layouts: 18.5 us -> 2.91 us
  starting transfers between devices: 3.53 us -> 12.2 us
  other arithmetic: 14.1 us -> 5.99 us
  matrix products: 6.03 us -> 0 us
  waiting for transfers between devices: 0.01 us -> 3.54 us
  between operations: 2.34 us -> 3.79 us
    all_gather x2 -> x0, blocking collectives: 18.9 us -> none  [the longest x1 13.1 us: local(): all_types = lax.all_gather(slot_kind[0], 'seq', axis=0, tiled=True)]
    pallas_call x0 -> x3, Pallas kernels: none -> 17.1 us  [the longest x2 15.3 us: encode(): pl.pallas_call(functools.partial(encode_kernel, ends, pack), out_shape=ou...]
    ppermute x1 -> x9, starting transfers between devices: 3.53 us -> 12.2 us  [the longest x8 10.2 us: exchange(): return lax.ppermute(value, axis, [(i, i ^ offset) for i in range(count)])]
    dot_general x3 -> x0, matrix products: 6.03 us -> none  [the longest x1 4.79 us: encode(): jnp.dot(columns.reshape(-1, 9 * channels), block_weight, preferred_elemen...]
    unnamed x1 -> x0, blocking collectives: 5.64 us -> none
    reduce_sum x12 -> x4, other arithmetic: 10.6 us -> 5.22 us  [live_excess(): return jnp.sum((kinds > 0).astype(jnp.int32)) - 2]
    convert_element_type x4 -> x0, local copies, waits for them, and re-layouts: 5.18 us -> none  [the longest x1 4.89 us: encode(): inner.astype(jnp.float32)]
    ppermute x1 -> x9, waiting for transfers between devices: 0.01 us -> 3.54 us  [the longest x8 3.53 us: exchange(): return lax.ppermute(value, axis, [(i, i ^ offset) for i in range(count)])]
  transfers between devices with their start and end apart: 1 -> 9, of which waited for: 0 -> 1; matrix products, arithmetic and copies ran while one was open for 8% -> 15% of each run, Pallas kernels for 0% -> 34%
where the time goes in v1:
time: 46.1 us; the launch traced here: 45.5 us
  Pallas kernels  17.1 us (37%)
  starting transfers between devices  12.2 us (26%)
  other arithmetic  5.99 us (13%)
  between operations  3.79 us (8%)
  waiting for transfers between devices  3.54 us (8%)
  local copies, waits for them, and re-layouts  2.91 us (6%)
    pallas_call x2, Pallas kernels, encode(): pl.pallas_call(functools.partial(encode_kernel, ends, pack), out_shape=ou...  15.3 us
    ppermute x8, starting transfers between devices, exchange(): return lax.ppermute(value, axis, [(i, i ^ offset) for i in range(count)])  10.2 us
    reduce_sum x4, other arithmetic, live_excess(): return jnp.sum((kinds > 0).astype(jnp.int32)) - 2  5.22 us
    ppermute x8, waiting for transfers between devices, exchange(): return lax.ppermute(value, axis, [(i, i ^ offset) for i in range(count)])  3.53 us
    unnamed x6, local copies, waits for them, and re-layouts  2.3 us
    ppermute x1, starting transfers between devices, swap_odd_pairs(): return lax.ppermute(value, axis, pairs)  2.03 us
    pallas_call x1, Pallas kernels, join(): pl.pallas_call(functools.partial(join_kernel, parts), out_shape=jax.Shape...  1.84 us
  transfers between devices with their start and end apart: 9, of which 1 were waited for; matrix products, arithmetic and copies ran while one was open for 15% of the time, Pallas kernels for 34%

profile of v1, /device:TPU:0, one launch (start us, length us, event | category | flops | bytes accessed | tf_op | source)
XLA Modules:
  0.0 45.5 jit_solution(9069647994359368213)
XLA Ops:
  0.0 5.0 %collective-permute-start.2 = (s32[1,3]{1,0:T(1,128)}, s32[1,3]{1,0:T(1,128)}, u32[]{:S(2)}, u32[]{:S(2)}) collective-permute-start(s32[1,3]{1,0:T(1,128)} %kind_hbm.3), channel_id=1, source_target_pairs={{0,6},{1,7},{2,4},{3,5},{4,2},{5,3},{6,0},{7,1},{8,14},{9,15},{10,... | collective-permute-start | bytes 44 | tf_op jit(solution)/shard_map/ppermute | solution.py:293
  5.0 0.0 collective-permute-start.1
  5.1 0.6 %collective-permute-start = (s32[1,3]{1,0:T(1,128)}, s32[1,3]{1,0:T(1,128)}, u32[]{:S(2)}, u32[]{:S(2)}) collective-permute-start(s32[1,3]{1,0:T(1,128)} %kind_hbm.3), channel_id=1, source_target_pairs={{0,2},{1,3},{2,0},{3,1},{4,6},{5,7},{6,4},{7,5},{8,10},{9,11},{10,... | collective-permute-start | bytes 44 | tf_op jit(solution)/shard_map/ppermute | solution.py:293
  5.6 8.9 %encode_0_1.1 = (bf16[2,64,64]{2,1,0:T(8,128)(2,1)}, bf16[80,288]{1,0:T(8,128)(2,1)}) custom-call(s32[1,3]{1,0:T(1,128)} %kind_hbm.3, bf16[1,768,512]{2,1,0:T(8,128)(2,1)} %feat_ref.3, bf16[4608,512]{1,0:T(8,128)(2,1)} %bw_ref.3, f32[512]{0:T(512)} %rest_0_.3, f32[512]{0:T(512)} %rest_1_.3, f32[512]{0:T(512)} %rest_2_.3, f32[512]{0:T(512)} %rest_3_.3, ...), custom_call_target="tpu_custom_call" | custom-call | flops 2491416576 | bytes 4718592 | tf_op jit(solution)/shard_map/encode_0_1/pallas_call | solution.py:223
  14.6 2.0 %collective-permute-start.5 = (bf16[2,64,64]{2,1,0:T(8,128)(2,1)}, bf16[2,64,64]{2,1,0:T(8,128)(2,1)}, u32[]{:S(2)}, u32[]{:S(2)}) collective-permute-start(bf16[2,64,64]{2,1,0:T(8,128)(2,1)} %get-tuple-element.7.own_ref), channel_id=1, source_target_pairs={{0,0},{7,7},{1,2},{2,1},{3,4},{4,3},{5,6},{6,5},{8,8},{15,15},{9,1... | collective-permute-start | bytes 49160 | tf_op jit(solution)/shard_map/ppermute | solution.py:301
  16.6 2.9 %collective-permute-start.4 = (bf16[2,64,64]{2,1,0:T(8,128)(2,1)}, bf16[2,64,64]{2,1,0:T(8,128)(2,1)}, u32[]{:S(2)}, u32[]{:S(2)}) collective-permute-start(bf16[2,64,64]{2,1,0:T(8,128)(2,1)} %get-tuple-element.7.own_ref), channel_id=1, source_target_pairs={{0,1},{1,0},{2,3},{3,2},{4,5},{5,4},{6,7},{7,6},{8,9},{9,8},{10,11... | collective-permute-start | bytes 49160 | tf_op jit(solution)/shard_map/ppermute | solution.py:293
  19.5 1.3 %fusion.3 = s32[]{:T(128)} fusion(s32[1,3]{1,0:T(1,128)} %kind_hbm.3), kind=kLoop, calls=%fused_computation.7 | loop fusion | flops 8 | bytes 16 | tf_op jit(solution)/shard_map/reduce_sum | solution.py:305
  20.8 6.3 %encode_2.1.third_ref = bf16[1,64,64]{2,1,0:T(8,128)(2,1)} custom-call(s32[1,3]{1,0:T(1,128)} %kind_hbm.3, bf16[1,768,512]{2,1,0:T(8,128)(2,1)} %feat_ref.3, bf16[4608,512]{1,0:T(8,128)(2,1)} %bw_ref.3, f32[512]{0:T(512)} %rest_0_.3, f32[512]{0:T(512)} %rest_1_.3, f32[512]{0:T(512)} %rest_2_.3, f32[512]{0:T(512)} %rest_3_.3, f32[512]{0:T(512)} %rest_4_.3, ...), custom_call_target="tpu_custom_call" | custom-call | flops 1245708288 | bytes 4718592 | tf_op jit(solution)/shard_map/encode_2/pallas_call | solution.py:223
  27.8 0.1 collective-permute-start.8
  27.9 1.3 %fusion.2 = s32[]{:T(128)} fusion(s32[1,3]{1,0:T(1,128)} %collective-permute-done.2), kind=kLoop, calls=%fused_computation.6 | loop fusion | flops 8 | bytes 16 | tf_op jit(solution)/shard_map/reduce_sum | solution.py:305
  29.9 1.6 %collective-permute-start.7 = (bf16[80,288]{1,0:T(8,128)(2,1)}, bf16[80,288]{1,0:T(8,128)(2,1)S(1)}, u32[]{:S(2)}, u32[]{:S(2)}) collective-permute-start(bf16[80,288]{1,0:T(8,128)(2,1)} %get-tuple-element.8.rest_0_), channel_id=1, source_target_pairs={{0,16},{8,24},{16,0},{24,8},{1,17},{9,25},{17,1},{25,9},{2,18},{10... | collective-permute-start | bytes 138248 | tf_op jit(solution)/shard_map/ppermute | solution.py:293
  31.4 1.3 %fusion.1 = s32[]{:T(128)} fusion(s32[1,3]{1,0:T(1,128)} %collective-permute-done.1), kind=kLoop, calls=%fused_computation.5 | loop fusion | flops 8 | bytes 16 | tf_op jit(solution)/shard_map/reduce_sum | solution.py:305
  33.4 1.3 %fusion = s32[]{:T(128)} fusion(s32[1,3]{1,0:T(1,128)} %collective-permute-done), kind=kLoop, calls=%fused_computation.4 | loop fusion | flops 8 | bytes 16 | tf_op jit(solution)/shard_map/reduce_sum | solution.py:305
  35.2 0.1 pad_add_fusion
  35.3 0.0 collective-permute-start.3
  35.3 3.5 %collective-permute-done.3 = s32[2]{0:T(128)S(1)} collective-permute-done((s32[2]{0:T(128)S(1)}, s32[2]{0:T(128)S(1)}, u32[]{:S(2)}, u32[]{:S(2)}) %collective-permute-start.3) | collective-permute-done | bytes 40 | tf_op jit(solution)/shard_map/ppermute | solution.py:293
  38.8 0.6 %fusion.4 = (s32[1]{0:T(128)}, s32[1]{0:T(128)}) fusion(s32[2]{0:T(128)S(1)} %collective-permute-done.3), kind=kLoop, calls=%fused_computation.10 | loop fusion | bytes 16 | tf_op jit(solution)/shard_map/slice | solution.py:326
  40.7 0.7 %pad_add_fusion.1.info_ref = s32[4]{0:T(128)S(1)} fusion(s32[1]{0:T(128)} %bitcast.7, s32[1]{0:T(128)} %bitcast.6, s32[1]{0:T(128)} %bitcast.5, s32[1]{0:T(128)} %bitcast.4), kind=kLoop, calls=%fused_computation.9 | loop fusion | flops 12 | bytes 32 | tf_op jit(solution)/shard_map/stack | solution.py:327
  41.4 0.0 collective-permute-done.5.odd_ref
  41.4 0.0 collective-permute-done.4.even_ref
  41.4 0.7 %copy-done = bf16[1,64,64]{2,1,0:T(8,128)(2,1)S(1)} copy-done((bf16[1,64,64]{2,1,0:T(8,128)(2,1)S(1)}, bf16[1,64,64]{2,1,0:T(8,128)(2,1)}, u32[]{:S(2)}) %copy-start) | copy-done | bytes 8216
  42.1 0.8 %copy-done.1 = bf16[80,288]{1,0:T(8,128)(2,1)S(1)} copy-done((bf16[80,288]{1,0:T(8,128)(2,1)S(1)}, bf16[80,288]{1,0:T(8,128)(2,1)}, u32[]{:S(2)}) %copy-start.1) | copy-done | bytes 46104
  42.9 0.8 %copy-done.2 = bf16[2,64,64]{2,1,0:T(8,128)(2,1)S(1)} copy-done((bf16[2,64,64]{2,1,0:T(8,128)(2,1)S(1)}, bf16[2,64,64]{2,1,0:T(8,128)(2,1)}, u32[]{:S(2)}) %copy-start.2) | copy-done | bytes 16408
  43.7 1.8 %join.1 = bf16[1,128,1152]{2,1,0:T(8,128)(2,1)} custom-call(s32[4]{0:T(128)S(1)} %pad_add_fusion.1.info_ref, bf16[2,64,64]{2,1,0:T(8,128)(2,1)S(1)} %copy-done.2, bf16[1,64,64]{2,1,0:T(8,128)(2,1)S(1)} %copy-done, bf16[2,64,64]{2,1,0:T(8,128)(2,1)} %collective-permute-done.4.even_ref, bf16[2,64,64]{2,1,0:T(8,128)(2,1)} %collective-permute-done.5.odd_ref, ...), custom_call_target="tpu_custom_call" | custom-call | flops 18874368 | bytes 294912 | tf_op jit(solution)/shard_map/join/pallas_call | solution.py:278
  (10 shorter events, 0.0 us)
Async XLA Ops:
  0.0 27.8 %collective-permute-start.2 = (s32[1,3]{1,0:T(1,128)}, s32[1,3]{1,0:T(1,128)}, u32[]{:S(2)}, u32[]{:S(2)}) collective-permute-start(s32[1,3]{1,0:T(1,128)} %kind_hbm.3), channel_id=1, source_target_pairs={{0,6},{1,7},{2,4},{3,5},{4,2},{5,3},{6,0},{7,1},{8,14},{9,15},{10,... | collective-permute-start | bytes 44 | tf_op jit(solution)/shard_map/ppermute | solution.py:293
  5.0 24.8 %collective-permute-start.1 = (s32[1,3]{1,0:T(1,128)}, s32[1,3]{1,0:T(1,128)}, u32[]{:S(2)}, u32[]{:S(2)}) collective-permute-start(s32[1,3]{1,0:T(1,128)} %kind_hbm.3), channel_id=1, source_target_pairs={{0,4},{1,5},{2,6},{3,7},{4,0},{5,1},{6,2},{7,3},{8,12},{9,13},{10,... | collective-permute-start | bytes 44 | tf_op jit(solution)/shard_map/ppermute | solution.py:293
  5.1 28.3 %collective-permute-start = (s32[1,3]{1,0:T(1,128)}, s32[1,3]{1,0:T(1,128)}, u32[]{:S(2)}, u32[]{:S(2)}) collective-permute-start(s32[1,3]{1,0:T(1,128)} %kind_hbm.3), channel_id=1, source_target_pairs={{0,2},{1,3},{2,0},{3,1},{4,6},{5,7},{6,4},{7,5},{8,10},{9,11},{10,... | collective-permute-start | bytes 44 | tf_op jit(solution)/shard_map/ppermute | solution.py:293
  14.6 26.8 %collective-permute-start.5 = (bf16[2,64,64]{2,1,0:T(8,128)(2,1)}, bf16[2,64,64]{2,1,0:T(8,128)(2,1)}, u32[]{:S(2)}, u32[]{:S(2)}) collective-permute-start(bf16[2,64,64]{2,1,0:T(8,128)(2,1)} %get-tuple-element.7.own_ref), channel_id=1, source_target_pairs={{0,0},{7,7},{1,2},{2,1},{3,4},{4,3},{5,6},{6,5},{8,8},{15,15},{9,1... | collective-permute-start | bytes 49160 | tf_op jit(solution)/shard_map/ppermute | solution.py:301
  16.6 24.8 %collective-permute-start.4 = (bf16[2,64,64]{2,1,0:T(8,128)(2,1)}, bf16[2,64,64]{2,1,0:T(8,128)(2,1)}, u32[]{:S(2)}, u32[]{:S(2)}) collective-permute-start(bf16[2,64,64]{2,1,0:T(8,128)(2,1)} %get-tuple-element.7.own_ref), channel_id=1, source_target_pairs={{0,1},{1,0},{2,3},{3,2},{4,5},{5,4},{6,7},{7,6},{8,9},{9,8},{10,11... | collective-permute-start | bytes 49160 | tf_op jit(solution)/shard_map/ppermute | solution.py:293
  27.8 13.6 %collective-permute-start.8 = (bf16[80,288]{1,0:T(8,128)(2,1)}, bf16[80,288]{1,0:T(8,128)(2,1)S(1)}, u32[]{:S(2)}, u32[]{:S(2)}) collective-permute-start(bf16[80,288]{1,0:T(8,128)(2,1)} %get-tuple-element.8.rest_0_), channel_id=1, source_target_pairs={{0,24},{8,16},{16,8},{24,0},{1,25},{9,17},{17,9},{25,1},{2,26},{10... | collective-permute-start | bytes 138248 | tf_op jit(solution)/shard_map/ppermute | solution.py:293
  29.9 11.5 %collective-permute-start.7 = (bf16[80,288]{1,0:T(8,128)(2,1)}, bf16[80,288]{1,0:T(8,128)(2,1)S(1)}, u32[]{:S(2)}, u32[]{:S(2)}) collective-permute-start(bf16[80,288]{1,0:T(8,128)(2,1)} %get-tuple-element.8.rest_0_), channel_id=1, source_target_pairs={{0,16},{8,24},{16,0},{24,8},{1,17},{9,25},{17,1},{25,9},{2,18},{10... | collective-permute-start | bytes 138248 | tf_op jit(solution)/shard_map/ppermute | solution.py:293
  35.3 3.5 %collective-permute-start.3 = (s32[2]{0:T(128)S(1)}, s32[2]{0:T(128)S(1)}, u32[]{:S(2)}, u32[]{:S(2)}) collective-permute-start(s32[2]{0:T(128)S(1)} %pad_add_fusion), channel_id=1, source_target_pairs={{0,1},{1,0},{2,3},{3,2},{4,5},{5,4},{6,7},{7,6},{8,9},{9,8},{10,11... | collective-permute-start | bytes 32 | tf_op jit(solution)/shard_map/ppermute | solution.py:293
  38.8 2.5 %collective-permute-start.6 = (bf16[80,288]{1,0:T(8,128)(2,1)}, bf16[80,288]{1,0:T(8,128)(2,1)S(1)}, u32[]{:S(2)}, u32[]{:S(2)}) collective-permute-start(bf16[80,288]{1,0:T(8,128)(2,1)} %get-tuple-element.8.rest_0_), channel_id=1, source_target_pairs={{0,8},{8,0},{16,24},{24,16},{1,9},{9,1},{17,25},{25,17},{2,10},{10... | collective-permute-start | bytes 138248 | tf_op jit(solution)/shard_map/ppermute | solution.py:293
  41.4 0.7 %copy-start = (bf16[1,64,64]{2,1,0:T(8,128)(2,1)S(1)}, bf16[1,64,64]{2,1,0:T(8,128)(2,1)}, u32[]{:S(2)}) copy-start(bf16[1,64,64]{2,1,0:T(8,128)(2,1)} %encode_2.1.third_ref) | copy-start | bytes 24580
  42.1 0.8 %copy-start.1 = (bf16[80,288]{1,0:T(8,128)(2,1)S(1)}, bf16[80,288]{1,0:T(8,128)(2,1)}, u32[]{:S(2)}) copy-start(bf16[80,288]{1,0:T(8,128)(2,1)} %get-tuple-element.8.rest_0_) | copy-start | bytes 138244
  42.9 0.8 %copy-start.2 = (bf16[2,64,64]{2,1,0:T(8,128)(2,1)S(1)}, bf16[2,64,64]{2,1,0:T(8,128)(2,1)}, u32[]{:S(2)}) copy-start(bf16[2,64,64]{2,1,0:T(8,128)(2,1)} %get-tuple-element.7.own_ref) | copy-start | bytes 49156

commit v2 on v1

v2 whole, which is shorter than its diff:
```python
import functools
import jax
import jax.numpy as jnp
from jax import lax
from jax.sharding import PartitionSpec as P
from jax.experimental import pallas as pl
from jax.experimental.pallas import tpu as pltpu

GROUPS = 32
SLOT_ROWS = 32
SLOT_COLS = 8
LATENT_SHIFT = 0.0609
LATENT_SCALE = 1.5305
NORM_EPSILON = 1e-06
LANES = 128
VMEM_BYTES = 64 * 1024 * 1024
F32 = jnp.float32
BF16 = jnp.bfloat16


def group_total(stats, same_group):
    rows, channels = stats.shape
    chunks = channels // LANES
    packed = jnp.concatenate([stats[:, k * LANES:(k + 1) * LANES] for k in range(chunks)], axis=0)
    high = packed.astype(BF16)
    rest = packed - high.astype(F32)
    middle = rest.astype(BF16)
    low = (rest - middle.astype(F32)).astype(BF16)
    total = sum(jnp.dot(piece, same_group, preferred_element_type=F32) for piece in (high, middle, low))
    return jnp.concatenate([total[k * rows:(k + 1) * rows] for k in range(chunks)], axis=1)


def affine(stats, joined, gain, shift, same_group, count):
    total = group_total(stats, same_group)
    mean, square = total[0:2] * (1.0 / count), total[2:4] * (1.0 / count)
    both_mean = 0.5 * (mean[0:1] + mean[1:2])
    both_square = 0.5 * (square[0:1] + square[1:2])
    mean = jnp.where(joined, both_mean, mean)
    square = jnp.where(joined, both_square, square)
    spread = jnp.maximum(square - mean * mean, 0.0)
    scale = lax.rsqrt(spread + NORM_EPSILON) * (0.5 * gain)
    return scale, 0.5 * shift - mean * scale


def half_stats(half):
    total = jnp.sum(half, axis=0, keepdims=True)
    return total, jnp.sum(half * half, axis=0, keepdims=True)


def norm_first(x_ref, joined, gain, shift, same_group, z_ref, u_ref):
    cells, channels = x_ref.shape
    half = cells // 2
    rows = cells // SLOT_COLS
    chunks = channels // LANES
    count = half * (channels // GROUPS)
    keep = jnp.where(joined, 1.0, 0.0).astype(F32)
    column = lax.broadcasted_iota(jnp.int32, (1, SLOT_COLS, 1), 1)
    parts = []
    for k in range(chunks):
        x = x_ref[:, k * LANES:(k + 1) * LANES].astype(F32)
        t0, q0 = half_stats(x[:half])
        t1, q1 = half_stats(x[half:])
        parts.append(jnp.concatenate([t0, t1, q0, q1], axis=0))
    scale, offset = affine(jnp.concatenate(parts, axis=1), joined, gain, shift, same_group, count)
    zero = jnp.zeros((SLOT_COLS, LANES), F32)
    for k in range(chunks):
        lanes = slice(k * LANES, (k + 1) * LANES)
        x = x_ref[:, lanes].astype(F32)
        v = jnp.concatenate([x[:half] * scale[0:1, lanes] + offset[0:1, lanes],
                             x[half:] * scale[1:2, lanes] + offset[1:2, lanes]], axis=0)
        act = v + v * jnp.tanh(v)
        act3 = act.reshape(rows, SLOT_COLS, LANES)
        left = jnp.where(column == 0, 0.0, pltpu.roll(act3, 1, 1)).reshape(cells, LANES)
        right = jnp.where(column == SLOT_COLS - 1, 0.0, pltpu.roll(act3, SLOT_COLS - 1, 1)).reshape(cells, LANES)
        for b, value in enumerate((left, act, right)):
            z_ref[b, :, lanes] = value.astype(BF16)
            over = value[half:half + SLOT_COLS] * keep
            under = value[half - SLOT_COLS:half] * keep
            u_ref[b, 0, :, lanes] = jnp.concatenate([zero, value[:half], over], axis=0).astype(BF16)
            u_ref[b, 1, :, lanes] = jnp.concatenate([under, value[half:], zero], axis=0).astype(BF16)


def conv(x_ref, bias, wbuf, wait_weights, z_ref, u_ref, y_ref):
    cells, channels = x_ref.shape
    half = cells // 2
    total = None
    for step, a in enumerate((0, -1, 1)):
        if a == 0:
            lhs = jnp.concatenate([z_ref[b] for b in range(3)], axis=1)
        else:
            first = 0 if a < 0 else 2 * SLOT_COLS
            lhs = jnp.concatenate(
                [jnp.concatenate([u_ref[b, h, first:first + half, :] for h in range(2)], axis=0) for b in range(3)],
                axis=1)
        wait_weights(step)
        depth = 3 * channels
        base = (a + 1) * depth
        term = jnp.dot(lhs, wbuf[base:base + depth, :], preferred_element_type=F32)
        total = term if total is None else total + term
    y_ref[...] = (x_ref[...].astype(F32) + (total + bias)).astype(BF16)


def norm_second(y_ref, joined, gain, shift, same_group):
    cells, channels = y_ref.shape
    half = cells // 2
    chunks = channels // LANES
    count = half * (channels // GROUPS)
    parts = []
    for k in range(chunks):
        lanes = slice(k * LANES, (k + 1) * LANES)
        inner = y_ref[:, lanes].astype(F32)
        t0, q0 = half_stats(inner[:half])
        t1, q1 = half_stats(inner[half:])
        parts.append(jnp.concatenate([t0, t1, q0, q1], axis=0))
    scale, offset = affine(jnp.concatenate(parts, axis=1), joined, gain, shift, same_group, count)
    for k in range(chunks):
        lanes = slice(k * LANES, (k + 1) * LANES)
        y = y_ref[:, lanes].astype(F32)
        v = jnp.concatenate([y[:half] * scale[0:1, lanes] + offset[0:1, lanes],
                             y[half:] * scale[1:2, lanes] + offset[1:2, lanes]], axis=0)
        y_ref[:, lanes] = (v + v * jnp.tanh(v)).astype(BF16)


def to_patches(y_ref, joined, lw_ref, bias, perm):
    cells, channels = y_ref.shape
    rows = cells // SLOT_COLS
    keep = jnp.where(joined, 1.0, 0.0).astype(F32)
    column = lax.broadcasted_iota(jnp.int32, (1, SLOT_COLS, 1), 1)
    lane = lax.broadcasted_iota(jnp.int32, (1, 1, 2 * LANES), 2)
    lat = lw_ref.shape[0] // 9
    lane_a, lane_b = lane // (3 * lat), (lane // lat) % 3
    taps = lax.dot_general(y_ref[...], lw_ref[...], (((1,), (1,)), ((), ())), preferred_element_type=F32)
    taps = jnp.concatenate([taps, jnp.zeros((cells, 2 * LANES - 9 * lat), F32)], axis=1).reshape(rows, SLOT_COLS, 2 * LANES)
    from_left = jnp.where(column == 0, 0.0, pltpu.roll(taps, 1, 1))
    from_right = jnp.where(column == SLOT_COLS - 1, 0.0, pltpu.roll(taps, SLOT_COLS - 1, 1))
    moved = jnp.where(lane_b == 0, from_left, jnp.where(lane_b == 1, taps, from_right))
    blank = jnp.zeros((1, SLOT_COLS, 2 * LANES), F32)
    mid = rows // 2
    above = jnp.concatenate([blank, moved[:mid - 1], moved[mid - 1:mid] * keep, moved[mid:rows - 1]], axis=0)
    below = jnp.concatenate([moved[1:mid], moved[mid:mid + 1] * keep, moved[mid + 1:], blank], axis=0)
    moved = jnp.where(lane_a == 0, above, jnp.where(lane_a == 1, moved, below)).reshape(cells, 2 * LANES)
    folded = moved[:, :LANES]
    width = LANES // 2
    while width >= lat:
        folded = folded + pltpu.roll(folded, width, 1)
        width //= 2
    latent = (folded + moved[:, LANES:])[:, :lat]
    latent = ((latent + bias) - LATENT_SHIFT) * LATENT_SCALE
    spread = jnp.dot(perm, latent.astype(BF16), preferred_element_type=F32)
    tokens = cells // 4
    return jnp.concatenate([spread[k * tokens:(k + 1) * tokens] for k in range(4)], axis=1).astype(BF16)


def group_table(channels):
    width = channels // GROUPS
    r = lax.broadcasted_iota(jnp.int32, (LANES, LANES), 0) // width
    c = lax.broadcasted_iota(jnp.int32, (LANES, LANES), 1) // width
    return jnp.where(r == c, 1.0, 0.0).astype(BF16)


def patch_table(cells):
    tokens = cells // 4
    half_cols = SLOT_COLS // 2
    row = lax.broadcasted_iota(jnp.int32, (cells, cells), 0)
    col = lax.broadcasted_iota(jnp.int32, (cells, cells), 1)
    block, token = row // tokens, row % tokens
    cell = (2 * (token // half_cols) + block // 2) * SLOT_COLS + 2 * (token % half_cols) + block % 2
    return jnp.where(cell == col, 1.0, 0.0).astype(BF16)


ENDS = 3


def vector(ref):
    return ref[...].reshape(1, ref.shape[0])


def begin_kernel(kind_hbm, feat_hbm, bw_hbm, ew_hbm, eb_hbm, *rest):
    names = 7
    small_hbm, rest = rest[:names], rest[names:]
    state_ref, x_ref, w_ref, perm_ref, piece_ref, out_ref, *rest = rest
    small, rest = rest[:names], rest[names:]
    kind_ref, ew_ref, eb_ref, z_ref, u_ref, y_ref, ksem, xsem, wsem, ssem = rest
    gain1, shift1, bias1, gain2, shift2, lw_ref, bias2 = small
    slots, cells, channels = x_ref.shape
    kcopy = pltpu.make_async_copy(kind_hbm, kind_ref, ksem)
    kcopy.start()
    xcopies = [pltpu.make_async_copy(feat_hbm.at[0, pl.ds(s * cells, cells), :], x_ref.at[s], xsem.at[s])
               for s in range(slots)]
    depth = 3 * channels
    wcopies = [pltpu.make_async_copy(
        bw_hbm.at[pl.ds((a + 1) * depth, depth), :], w_ref.at[pl.ds((a + 1) * depth, depth), :], wsem.at[i])
        for i, a in enumerate((0, -1, 1))]
    scopies = [pltpu.make_async_copy(src, dst, ssem.at[i])
               for i, (src, dst) in enumerate(zip(small_hbm + (ew_hbm, eb_hbm), small + [ew_ref, eb_ref]))]
    for c in xcopies + scopies + wcopies:
        c.start()
    perm_ref[...] = patch_table(cells)
    same_group = group_table(channels)
    kcopy.wait()
    live = jnp.int32(0)
    for s in range(slots):
        live = live + jnp.where(kind_ref[0, s] > 0, 1, 0).astype(jnp.int32)
    state_ref[0] = live
    for end in range(ENDS):
        slot = jnp.maximum(live - 1 - end, 0)
        state_ref[1 + end] = slot
        state_ref[1 + ENDS + end] = kind_ref[0, slot]
    for c in scopies + xcopies:
        c.wait()
    feats = ew_ref.shape[0]
    piece_ref[0:feats, :] = ew_ref[...]
    piece_ref[feats:, :] = jnp.broadcast_to(vector(eb_ref), (piece_ref.shape[0] - feats, ew_ref.shape[1]))
    x = x_ref.at[state_ref[1]]
    joined = state_ref[1 + ENDS] == 2
    norm_first(x, joined, vector(gain1), vector(shift1), same_group, z_ref, u_ref)
    conv(x, vector(bias1), w_ref, lambda step: wcopies[step].wait(), z_ref, u_ref, y_ref)
    norm_second(y_ref, joined, vector(gain2), vector(shift2), same_group)
    out_ref[...] = to_patches(y_ref, joined, lw_ref, vector(bias2), perm_ref[...])


def encode_end(end, state_ref, x_ref, w_ref, perm_ref, small, scratch):
    gain1, shift1, bias1, gain2, shift2, lw_ref, bias2 = small
    z_ref, u_ref, y_ref = scratch
    same_group = group_table(x_ref.shape[2])
    x = x_ref.at[state_ref[1 + end]]
    joined = state_ref[1 + ENDS + end] == 2
    norm_first(x, joined, vector(gain1), vector(shift1), same_group, z_ref, u_ref)
    conv(x, vector(bias1), w_ref, lambda step: None, z_ref, u_ref, y_ref)
    norm_second(y_ref, joined, vector(gain2), vector(shift2), same_group)
    return to_patches(y_ref, joined, lw_ref, vector(bias2), perm_ref[...])


def count_live(kind_ref):
    total = jnp.int32(-2)
    for s in range(kind_ref.shape[1]):
        total = total + jnp.where(kind_ref[0, s] > 0, 1, 0).astype(jnp.int32)
    return total


def middle_kernel(offsets, state_ref, x_ref, w_ref, perm_ref, last_ref, *rest):
    names = 7
    small, rest = rest[:names], rest[names:]
    others, rest = rest[:len(offsets)], rest[len(offsets):]
    message_ref, sums_ref, *rest = rest
    scratch, rest = rest[:3], rest[3:]
    kinds, ksem = rest[:-1], rest[-1]
    copies = [pltpu.make_async_copy(src, dst, ksem.at[i]) for i, (src, dst) in enumerate(zip(others, kinds))]
    for c in copies:
        c.start()
    tokens, feats = last_ref.shape
    message_ref[0:tokens, :] = last_ref[...]
    message_ref[tokens:2 * tokens, :] = encode_end(1, state_ref, x_ref, w_ref, perm_ref, small, scratch)
    for c in copies:
        c.wait()
    position = lax.axis_index("seq")
    mine = state_ref[0] - 2
    below, above = jnp.int32(0), mine
    for offset, kind_ref in zip(offsets, kinds):
        other = count_live(kind_ref)
        lower = (position ^ offset) < position
        below = below + jnp.where(lower, other, 0)
        above = above + jnp.where(lower, 0, other)
    first_half = position < lax.axis_size("seq") // 2
    passed = jnp.where(position % 2 == 0, mine, 0)
    sums_ref[0] = jnp.where(first_half, below, -above)
    told = jnp.where(first_half, below + passed, passed - above)
    message_ref[2 * tokens:, :] = jnp.full((message_ref.shape[0] - 2 * tokens, feats), told.astype(F32)).astype(BF16)


def final_kernel(state_ref, x_ref, w_ref, perm_ref, *rest):
    small, rest = rest[:7], rest[7:]
    out_ref, *scratch = rest

    @pl.when(state_ref[0] > 2)
    def _():
        out_ref[...] = encode_end(2, state_ref, x_ref, w_ref, perm_ref, small, scratch)

    @pl.when(state_ref[0] <= 2)
    def _():
        out_ref[...] = jnp.zeros_like(out_ref)


def join_kernel(parts, state_ref, sums_ref, own_ref, third_ref, even_ref, odd_ref, *rest):
    pieces, out_ref, embed_ref, source_ref = rest[:parts], *rest[parts:]
    live = state_ref[0]
    group, position = lax.axis_index("dp"), lax.axis_index("seq")
    odd = position % 2
    tokens, feats = third_ref.shape
    width = pieces[0].shape[1]
    told = even_ref[2 * tokens:, :].astype(F32)[0, 0].astype(jnp.int32)
    carry = sums_ref[0] + told
    for j in range(parts):
        value = pieces[0][...]
        for k in range(1, parts):
            value = jnp.where((group ^ j) == k, pieces[k][...], value)
        embed_ref[:, j * width:(j + 1) * width] = value
    for k, ref in enumerate((even_ref, odd_ref, own_ref)):
        source_ref[2 * k] = ref[0:tokens, :]
        source_ref[2 * k + 1] = ref[tokens:2 * tokens, :]
    source_ref[6] = third_ref[...]
    weight = embed_ref[0:feats, :]
    bias = embed_ref[feats:feats + 1, :].astype(F32)
    for i in range(2):
        incoming = (1 - odd) * 2 + carry - 1 - i
        kept = 4 + live - 1 - (i - carry)
        patch = source_ref[jnp.clip(jnp.where(i < carry, incoming, kept), 0, 6)]
        value = jnp.dot(patch, weight, preferred_element_type=F32) + bias
        out_ref[0, i * tokens:(i + 1) * tokens, :] = value.astype(BF16)


def exchange(value, axis, offset):
    count = lax.axis_size(axis)
    return lax.ppermute(value, axis, [(i, i ^ offset) for i in range(count)])


def swap_odd_pairs(value, axis):
    count = lax.axis_size(axis)
    pairs = [(0, 0), (count - 1, count - 1)]
    for i in range(1, count - 1, 2):
        pairs += [(i, i + 1), (i + 1, i)]
    return lax.ppermute(value, axis, pairs)


VMEM_SPEC = pl.BlockSpec(memory_space=pltpu.VMEM)
SMEM_SPEC = pl.BlockSpec(memory_space=pltpu.SMEM)
ANY_SPEC = pl.BlockSpec(memory_space=pl.ANY)
MIB = 1024 * 1024


def cost(flops, moved):
    return pl.CostEstimate(flops=flops, bytes_accessed=moved, transcendentals=0)


def local(features, slot_kind, block_gain, block_shift, block_weight, block_bias, final_gain, final_shift,
          latent_weight, latent_bias, embed_weight, embed_bias):
    seq, dp = lax.axis_size("seq"), lax.axis_size("dp")
    slots = slot_kind.shape[1]
    channels = features.shape[2]
    cells = SLOT_ROWS * SLOT_COLS
    tokens = cells // 4
    feats, width = embed_weight.shape
    small = (block_gain, block_shift, block_bias, final_gain, final_shift, latent_weight.T, latent_bias)
    offsets = tuple(range(2, seq // 2, 2))
    others = [exchange(slot_kind, "seq", offset) for offset in offsets]
    buffers = [
        pltpu.VMEM((3, cells, channels), BF16),
        pltpu.VMEM((3, 2, cells // 2 + 2 * SLOT_COLS, channels), BF16),
        pltpu.VMEM((cells, channels), BF16),
    ]
    flops = cells * channels * 2 * 9 * (channels + latent_weight.shape[1] // 9)
    state, x, w, perm, piece, last, *small = pl.pallas_call(
        begin_kernel,
        out_shape=[
            pltpu.SMEM((8,), jnp.int32),
            pltpu.VMEM((slots, cells, channels), BF16),
            pltpu.VMEM(block_weight.shape, BF16),
            pltpu.VMEM((cells, cells), BF16),
            jax.ShapeDtypeStruct((feats + 16, width), BF16),
            pltpu.VMEM((tokens, feats), BF16),
        ] + [pltpu.VMEM(v.shape, v.dtype) for v in small],
        in_specs=[ANY_SPEC] * (5 + len(small)),
        out_specs=[SMEM_SPEC] + [VMEM_SPEC] * (5 + len(small)),
        scratch_shapes=[
            pltpu.SMEM(slot_kind.shape, jnp.int32),
            pltpu.VMEM(embed_weight.shape, BF16),
            pltpu.VMEM(embed_bias.shape, BF16),
        ] + buffers + [
            pltpu.SemaphoreType.DMA,
            pltpu.SemaphoreType.DMA((slots,)),
            pltpu.SemaphoreType.DMA((3,)),
            pltpu.SemaphoreType.DMA((len(small) + 2,)),
        ],
        compiler_params=pltpu.CompilerParams(vmem_limit_bytes=55 * MIB),
        cost_estimate=cost(flops, block_weight.size * 2),
        name="begin",
    )(slot_kind, features, block_weight, embed_weight, embed_bias, *small)
    message, sums = pl.pallas_call(
        functools.partial(middle_kernel, offsets),
        out_shape=[jax.ShapeDtypeStruct((2 * tokens + 16, feats), BF16), pltpu.SMEM((1,), jnp.int32)],
        in_specs=[SMEM_SPEC] + [VMEM_SPEC] * (4 + len(small)) + [ANY_SPEC] * len(others),
        out_specs=[VMEM_SPEC, SMEM_SPEC],
        scratch_shapes=buffers + [pltpu.SMEM(slot_kind.shape, jnp.int32) for _ in others]
        + [pltpu.SemaphoreType.DMA((len(others),))],
        compiler_params=pltpu.CompilerParams(vmem_limit_bytes=24 * MIB),
        cost_estimate=cost(flops, block_weight.size * 2),
        name="middle",
    )(state, x, w, perm, last, *small, *others)
    even = exchange(message, "seq", 1)
    odd = swap_odd_pairs(message, "seq")
    pieces = [piece] + [exchange(piece, "dp", offset) for offset in range(1, dp)]
    third = pl.pallas_call(
        final_kernel,
        out_shape=pltpu.VMEM((tokens, feats), BF16),
        in_specs=[SMEM_SPEC] + [VMEM_SPEC] * (3 + len(small)),
        out_specs=VMEM_SPEC,
        scratch_shapes=buffers,
        compiler_params=pltpu.CompilerParams(vmem_limit_bytes=24 * MIB),
        cost_estimate=cost(flops, block_weight.size * 2),
        name="final",
    )(state, x, w, perm, *small)
    return pl.pallas_call(
        functools.partial(join_kernel, dp),
        out_shape=jax.ShapeDtypeStruct((1, 2 * tokens, dp * width), BF16),
        in_specs=[SMEM_SPEC] * 2 + [VMEM_SPEC] * (4 + dp),
        out_specs=VMEM_SPEC,
        scratch_shapes=[pltpu.VMEM((feats + 16, dp * width), BF16), pltpu.VMEM((7, tokens, feats), BF16)],
        compiler_params=pltpu.CompilerParams(vmem_limit_bytes=8 * MIB),
        cost_estimate=cost(4 * tokens * feats * dp * width, 4 * tokens * dp * width),
        name="join",
    )(state, sums, message, third, even, odd, *pieces)


def solution(mesh):
    in_specs = (P("dp", "seq", None), P("dp", "seq")) + (P(),) * 8 + (P(None, "dp"), P("dp"))
    return jax.shard_map(local, mesh=mesh, in_specs=in_specs, out_specs=P("dp", "seq", None), check_vma=False)
```

time: 46.1 us -> 22.7 us (0.49)
  the two profiles are of different devices: /device:TPU:0 before, /device:TPU:16 now
where the time goes in v2:
time: 22.7 us; the launch traced here: 22.5 us
  Pallas kernels  13.5 us (59%)
  starting transfers between devices  6.98 us (31%)
  waiting for transfers between devices  2.01 us (9%)
    pallas_call x1, Pallas kernels, local(): pl.pallas_call(begin_kernel, out_shape=[pltpu.SMEM((8,), jnp.int32), pltp...  6.56 us
    ppermute x5, starting transfers between devices, exchange(): return lax.ppermute(value, axis, [(i, i ^ offset) for i in range(count)])  5.07 us
    pallas_call x1, Pallas kernels, local(): pl.pallas_call(functools.partial(middle_kernel, offsets), out_shape=[jax....  3.04 us
    pallas_call x1, Pallas kernels, local(): pl.pallas_call(final_kernel, out_shape=pltpu.VMEM((tokens, feats), BF16),...  2.8 us
    ppermute x1, waiting for transfers between devices, swap_odd_pairs(): return lax.ppermute(value, axis, pairs)  2 us
    ppermute x1, starting transfers between devices, swap_odd_pairs(): return lax.ppermute(value, axis, pairs)  1.91 us
    pallas_call x1, Pallas kernels, local(): pl.pallas_call(functools.partial(join_kernel, dp), out_shape=jax.ShapeDty...  1.08 us
  transfers between devices with their start and end apart: 6, of which 1 were waited for; matrix products, arithmetic and copies ran while one was open for 0% of the time, Pallas kernels for 55%

profile of v2, /device:TPU:16, one launch (start us, length us, event | category | flops | bytes accessed | tf_op | source)
XLA Modules:
  0.0 22.5 jit_solution(2400510170476536152)
XLA Ops:
  0.0 1.6 %collective-permute-start = (s32[1,3]{1,0:T(1,128)}, s32[1,3]{1,0:T(1,128)S(1)}, u32[]{:S(2)}, u32[]{:S(2)}) collective-permute-start(s32[1,3]{1,0:T(1,128)} %kind_hbm.1), channel_id=1, source_target_pairs={{0,2},{1,3},{2,0},{3,1},{4,6},{5,7},{6,4},{7,5},{8,10},{9,11},{10,... | collective-permute-start | bytes 44 | tf_op jit(solution)/shard_map/ppermute | solution.py:314
  1.6 6.6 %begin.1 = (s32[8]{0:T(128)S(4)}, bf16[3,256,512]{2,1,0:T(8,128)(2,1)S(1)}, bf16[4608,512]{1,0:T(8,128)(2,1)S(1)}, bf16[256,256]{1,0:T(8,128)(2,1)S(1)}, bf16[80...) custom-call(s32[1,3]{1,0:T(1,128)} %kind_hbm.1, ...), custom_call_target="tpu_custom_call" | custom-call | flops 1245708288 | bytes 4718592 | tf_op jit(solution)/shard_map/begin/pallas_call | solution.py:352
  8.1 0.1 collective-permute-start.3
  8.2 1.6 %collective-permute-start.4 = (bf16[80,288]{1,0:T(8,128)(2,1)}, bf16[80,288]{1,0:T(8,128)(2,1)S(1)}, u32[]{:S(2)}, u32[]{:S(2)}) collective-permute-start(bf16[80,288]{1,0:T(8,128)(2,1)} %get-tuple-element.34.rest_0_), channel_id=1, source_target_pairs={{0,16},{8,24},{16,0},{24,8},{1,17},{9,25},{17,1},{25,9},{2,18},{10... | collective-permute-start | bytes 138248 | tf_op jit(solution)/shard_map/ppermute | solution.py:314
  9.8 0.3 %collective-permute-start.5 = (bf16[80,288]{1,0:T(8,128)(2,1)}, bf16[80,288]{1,0:T(8,128)(2,1)S(1)}, u32[]{:S(2)}, u32[]{:S(2)}) collective-permute-start(bf16[80,288]{1,0:T(8,128)(2,1)} %get-tuple-element.34.rest_0_), channel_id=1, source_target_pairs={{0,24},{8,16},{16,8},{24,0},{1,25},{9,17},{17,9},{25,1},{2,26},{10... | collective-permute-start | bytes 138248 | tf_op jit(solution)/shard_map/ppermute | solution.py:314
  10.1 0.0 collective-permute-done.rest_7_
  10.1 0.0 copy-start
  10.1 3.0 %middle.1 = (bf16[144,64]{1,0:T(8,128)(2,1)S(1)}, s32[1]{0:T(128)S(4)}) custom-call(s32[8]{0:T(128)S(4)} %get-tuple-element.20.state_ref, bf16[3,256,512]{2,1,0:T(8,128)(2,1)S(1)} %get-tuple-element.21.x_ref, bf16[4608,512]{1,0:T(8,128)(2,1)S(1)} %get-tuple-element.22.w_ref, bf16[256,256]{1,0:T(8,128)(2,1)S(1)} %get-tuple-element.23.perm_ref, ...), custom_call_target="tpu_custom_call" | custom-call | flops 1245708288 | bytes 4718592 | tf_op jit(solution)/shard_map/middle/pallas_call | solution.py:378
  13.1 1.6 %collective-permute-start.1 = (bf16[144,64]{1,0:T(8,128)(2,1)S(1)}, bf16[144,64]{1,0:T(8,128)(2,1)S(1)}, u32[]{:S(2)}, u32[]{:S(2)}) collective-permute-start(bf16[144,64]{1,0:T(8,128)(2,1)S(1)} %get-tuple-element.33.own_ref), channel_id=1, source_target_pairs={{0,1},{1,0},{2,3},{3,2},{4,5},{5,4},{6,7},{7,6},{8,9},{9,8},{10,11... | collective-permute-start | bytes 55304 | tf_op jit(solution)/shard_map/ppermute | solution.py:314
  14.7 1.9 %collective-permute-start.2 = (bf16[144,64]{1,0:T(8,128)(2,1)S(1)}, bf16[144,64]{1,0:T(8,128)(2,1)S(1)}, u32[]{:S(2)}, u32[]{:S(2)}) collective-permute-start(bf16[144,64]{1,0:T(8,128)(2,1)S(1)} %get-tuple-element.33.own_ref), channel_id=1, source_target_pairs={{0,0},{7,7},{1,2},{2,1},{3,4},{4,3},{5,6},{6,5},{8,8},{15,15},{9,1... | collective-permute-start | bytes 55304 | tf_op jit(solution)/shard_map/ppermute | solution.py:322
  16.6 2.8 %final.1.third_ref = bf16[64,64]{1,0:T(8,128)(2,1)S(1)} custom-call(s32[8]{0:T(128)S(4)} %get-tuple-element.20.state_ref, bf16[3,256,512]{2,1,0:T(8,128)(2,1)S(1)} %get-tuple-element.21.x_ref, bf16[4608,512]{1,0:T(8,128)(2,1)S(1)} %get-tuple-element.22.w_ref, bf16[256,256]{1,0:T(8,128)(2,1)S(1)} %get-tuple-element.23.perm_ref, ...), custom_call_target="tpu_custom_call" | custom-call | flops 1245708288 | bytes 4718592 | tf_op jit(solution)/shard_map/final/pallas_call | solution.py:392
  19.4 0.0 collective-permute-done.1.even_ref
  19.4 2.0 %collective-permute-done.2.odd_ref = bf16[144,64]{1,0:T(8,128)(2,1)S(1)} collective-permute-done((bf16[144,64]{1,0:T(8,128)(2,1)S(1)}, bf16[144,64]{1,0:T(8,128)(2,1)S(1)}, u32[]{:S(2)}, u32[]{:S(2)}) %collective-permute-start.2) | collective-permute-done | bytes 18464 | tf_op jit(solution)/shard_map/ppermute | solution.py:322
  21.4 0.0 collective-permute-done.3.rest_1_
  21.4 0.0 collective-permute-done.4.rest_2_
  21.4 0.0 collective-permute-done.5.rest_3_
  21.4 0.0 copy-done
  21.5 1.1 %join.1 = bf16[1,128,1152]{2,1,0:T(8,128)(2,1)} custom-call(s32[8]{0:T(128)S(4)} %get-tuple-element.20.state_ref, s32[1]{0:T(128)S(4)} %get-tuple-element.32.sums_ref, bf16[144,64]{1,0:T(8,128)(2,1)S(1)} %get-tuple-element.33.own_ref, bf16[64,64]{1,0:T(8,128)(2,1)S(1)} %final.1.third_ref, bf16[144,64]{1,0:T(8,128)(2,1)S(1)} %collective-permute-done.1.even_ref, ...), custom_call_target="tpu_custom_call" | custom-call | flops 18874368 | bytes 294912 | tf_op jit(solution)/shard_map/join/pallas_call | solution.py:402
Async XLA Ops:
  0.0 10.1 %collective-permute-start = (s32[1,3]{1,0:T(1,128)}, s32[1,3]{1,0:T(1,128)S(1)}, u32[]{:S(2)}, u32[]{:S(2)}) collective-permute-start(s32[1,3]{1,0:T(1,128)} %kind_hbm.1), channel_id=1, source_target_pairs={{0,2},{1,3},{2,0},{3,1},{4,6},{5,7},{6,4},{7,5},{8,10},{9,11},{10,... | collective-permute-start | bytes 44 | tf_op jit(solution)/shard_map/ppermute | solution.py:314
  8.1 13.3 %collective-permute-start.3 = (bf16[80,288]{1,0:T(8,128)(2,1)}, bf16[80,288]{1,0:T(8,128)(2,1)S(1)}, u32[]{:S(2)}, u32[]{:S(2)}) collective-permute-start(bf16[80,288]{1,0:T(8,128)(2,1)} %get-tuple-element.34.rest_0_), channel_id=1, source_target_pairs={{0,8},{8,0},{16,24},{24,16},{1,9},{9,1},{17,25},{25,17},{2,10},{10... | collective-permute-start | bytes 138248 | tf_op jit(solution)/shard_map/ppermute | solution.py:314
  8.2 13.2 %collective-permute-start.4 = (bf16[80,288]{1,0:T(8,128)(2,1)}, bf16[80,288]{1,0:T(8,128)(2,1)S(1)}, u32[]{:S(2)}, u32[]{:S(2)}) collective-permute-start(bf16[80,288]{1,0:T(8,128)(2,1)} %get-tuple-element.34.rest_0_), channel_id=1, source_target_pairs={{0,16},{8,24},{16,0},{24,8},{1,17},{9,25},{17,1},{25,9},{2,18},{10... | collective-permute-start | bytes 138248 | tf_op jit(solution)/shard_map/ppermute | solution.py:314
  9.8 11.6 %collective-permute-start.5 = (bf16[80,288]{1,0:T(8,128)(2,1)}, bf16[80,288]{1,0:T(8,128)(2,1)S(1)}, u32[]{:S(2)}, u32[]{:S(2)}) collective-permute-start(bf16[80,288]{1,0:T(8,128)(2,1)} %get-tuple-element.34.rest_0_), channel_id=1, source_target_pairs={{0,24},{8,16},{16,8},{24,0},{1,25},{9,17},{17,9},{25,1},{2,26},{10... | collective-permute-start | bytes 138248 | tf_op jit(solution)/shard_map/ppermute | solution.py:314
  10.1 11.4 %copy-start = (bf16[80,288]{1,0:T(8,128)(2,1)S(1)}, bf16[80,288]{1,0:T(8,128)(2,1)}, u32[]{:S(2)}) copy-start(bf16[80,288]{1,0:T(8,128)(2,1)} %get-tuple-element.34.rest_0_) | copy-start | bytes 138244
  13.1 6.3 %collective-permute-start.1 = (bf16[144,64]{1,0:T(8,128)(2,1)S(1)}, bf16[144,64]{1,0:T(8,128)(2,1)S(1)}, u32[]{:S(2)}, u32[]{:S(2)}) collective-permute-start(bf16[144,64]{1,0:T(8,128)(2,1)S(1)} %get-tuple-element.33.own_ref), channel_id=1, source_target_pairs={{0,1},{1,0},{2,3},{3,2},{4,5},{5,4},{6,7},{7,6},{8,9},{9,8},{10,11... | collective-permute-start | bytes 55304 | tf_op jit(solution)/shard_map/ppermute | solution.py:314
  14.7 6.7 %collective-permute-start.2 = (bf16[144,64]{1,0:T(8,128)(2,1)S(1)}, bf16[144,64]{1,0:T(8,128)(2,1)S(1)}, u32[]{:S(2)}, u32[]{:S(2)}) collective-permute-start(bf16[144,64]{1,0:T(8,128)(2,1)S(1)} %get-tuple-element.33.own_ref), channel_id=1, source_target_pairs={{0,0},{7,7},{1,2},{2,1},{3,4},{4,3},{5,6},{6,5},{8,8},{15,15},{9,1... | collective-permute-start | bytes 55304 | tf_op jit(solution)/shard_map/ppermute | solution.py:322

commit v3 on v2

--- a/solution.py
+++ b/solution.py
@@ -128,7 +128,9 @@
     column = lax.broadcasted_iota(jnp.int32, (1, SLOT_COLS, 1), 1)
     lane = lax.broadcasted_iota(jnp.int32, (1, 1, 2 * LANES), 2)
     lat = lw_ref.shape[0] // 9
-    lane_a, lane_b = lane // (3 * lat), (lane // lat) % 3
+    tap = whole(lane, lat)
+    lane_a = jnp.where(tap < 3, 0, jnp.where(tap < 6, 1, 2))
+    lane_b = tap - 3 * lane_a
     taps = lax.dot_general(y_ref[...], lw_ref[...], (((1,), (1,)), ((), ())), preferred_element_type=F32)
     taps = jnp.concatenate([taps, jnp.zeros((cells, 2 * LANES - 9 * lat), F32)], axis=1).reshape(rows, SLOT_COLS, 2 * LANES)
     from_left = jnp.where(column == 0, 0.0, pltpu.roll(taps, 1, 1))
@@ -151,10 +153,18 @@
     return jnp.concatenate([spread[k * tokens:(k + 1) * tokens] for k in range(4)], axis=1).astype(BF16)
 
 
+def whole(value, size):
+    return value >> (size.bit_length() - 1)
+
+
+def part(value, size):
+    return value & (size - 1)
+
+
 def group_table(channels):
     width = channels // GROUPS
-    r = lax.broadcasted_iota(jnp.int32, (LANES, LANES), 0) // width
-    c = lax.broadcasted_iota(jnp.int32, (LANES, LANES), 1) // width
+    r = whole(lax.broadcasted_iota(jnp.int32, (LANES, LANES), 0), width)
+    c = whole(lax.broadcasted_iota(jnp.int32, (LANES, LANES), 1), width)
     return jnp.where(r == c, 1.0, 0.0).astype(BF16)
 
 
@@ -163,12 +173,12 @@
     half_cols = SLOT_COLS // 2
     row = lax.broadcasted_iota(jnp.int32, (cells, cells), 0)
     col = lax.broadcasted_iota(jnp.int32, (cells, cells), 1)
-    block, token = row // tokens, row % tokens
-    cell = (2 * (token // half_cols) + block // 2) * SLOT_COLS + 2 * (token % half_cols) + block % 2
+    block, token = whole(row, tokens), part(row, tokens)
+    cell = (2 * whole(token, half_cols) + whole(block, 2)) * SLOT_COLS + 2 * part(token, half_cols) + part(block, 2)
     return jnp.where(cell == col, 1.0, 0.0).astype(BF16)
 
 
-ENDS = 3
+FIRST = 1
 
 
 def vector(ref):
@@ -193,7 +203,8 @@
         for i, a in enumerate((0, -1, 1))]
     scopies = [pltpu.make_async_copy(src, dst, ssem.at[i])
                for i, (src, dst) in enumerate(zip(small_hbm + (ew_hbm, eb_hbm), small + [ew_ref, eb_ref]))]
-    for c in xcopies + scopies + wcopies:
+    xcopies[FIRST].start()
+    for c in scopies + wcopies + [c for k, c in enumerate(xcopies) if k != FIRST]:
         c.start()
     perm_ref[...] = patch_table(cells)
     same_group = group_table(channels)
@@ -201,30 +212,33 @@
     live = jnp.int32(0)
     for s in range(slots):
         live = live + jnp.where(kind_ref[0, s] > 0, 1, 0).astype(jnp.int32)
+    second = jnp.where(live > 2, 2, 0)
     state_ref[0] = live
-    for end in range(ENDS):
-        slot = jnp.maximum(live - 1 - end, 0)
-        state_ref[1 + end] = slot
-        state_ref[1 + ENDS + end] = kind_ref[0, slot]
-    for c in scopies + xcopies:
+    state_ref[1] = second
+    state_ref[2] = kind_ref[0, second]
+    state_ref[3] = kind_ref[0, 0]
+    for c in scopies + [xcopies[FIRST]]:
         c.wait()
     feats = ew_ref.shape[0]
     piece_ref[0:feats, :] = ew_ref[...]
     piece_ref[feats:, :] = jnp.broadcast_to(vector(eb_ref), (piece_ref.shape[0] - feats, ew_ref.shape[1]))
-    x = x_ref.at[state_ref[1]]
-    joined = state_ref[1 + ENDS] == 2
+    x = x_ref.at[FIRST]
+    joined = kind_ref[0, FIRST] == 2
     norm_first(x, joined, vector(gain1), vector(shift1), same_group, z_ref, u_ref)
     conv(x, vector(bias1), w_ref, lambda step: wcopies[step].wait(), z_ref, u_ref, y_ref)
     norm_second(y_ref, joined, vector(gain2), vector(shift2), same_group)
     out_ref[...] = to_patches(y_ref, joined, lw_ref, vector(bias2), perm_ref[...])
-
-
-def encode_end(end, state_ref, x_ref, w_ref, perm_ref, small, scratch):
+    for k, c in enumerate(xcopies):
+        if k != FIRST:
+            c.wait()
+
+
+def encode_slot(slot, kind, state_ref, x_ref, w_ref, perm_ref, small, scratch):
     gain1, shift1, bias1, gain2, shift2, lw_ref, bias2 = small
     z_ref, u_ref, y_ref = scratch
     same_group = group_table(x_ref.shape[2])
-    x = x_ref.at[state_ref[1 + end]]
-    joined = state_ref[1 + ENDS + end] == 2
+    x = x_ref.at[slot]
+    joined = kind == 2
     norm_first(x, joined, vector(gain1), vector(shift1), same_group, z_ref, u_ref)
     conv(x, vector(bias1), w_ref, lambda step: None, z_ref, u_ref, y_ref)
     norm_second(y_ref, joined, vector(gain2), vector(shift2), same_group)
@@ -249,8 +263,10 @@
     for c in copies:
         c.start()
     tokens, feats = last_ref.shape
-    message_ref[0:tokens, :] = last_ref[...]
-    message_ref[tokens:2 * tokens, :] = encode_end(1, state_ref, x_ref, w_ref, perm_ref, small, scratch)
+    first_at = pl.multiple_of(jnp.where(state_ref[0] == 2, 0, tokens), tokens)
+    message_ref[pl.ds(first_at, tokens), :] = last_ref[...]
+    message_ref[pl.ds(tokens - first_at, tokens), :] = encode_slot(
+        state_ref[1], state_ref[2], state_ref, x_ref, w_ref, perm_ref, small, scratch)
     for c in copies:
         c.wait()
     position = lax.axis_index("seq")
@@ -274,7 +290,7 @@
 
     @pl.when(state_ref[0] > 2)
     def _():
-        out_ref[...] = encode_end(2, state_ref, x_ref, w_ref, perm_ref, small, scratch)
+        out_ref[...] = encode_slot(0, state_ref[3], state_ref, x_ref, w_ref, perm_ref, small, scratch)
 
     @pl.when(state_ref[0] <= 2)
     def _():
@@ -314,12 +330,14 @@
     return lax.ppermute(value, axis, [(i, i ^ offset) for i in range(count)])
 
 
-def swap_odd_pairs(value, axis):
-    count = lax.axis_size(axis)
-    pairs = [(0, 0), (count - 1, count - 1)]
-    for i in range(1, count - 1, 2):
-        pairs += [(i, i + 1), (i + 1, i)]
-    return lax.ppermute(value, axis, pairs)
+def swap_odd_pairs(value):
+    groups, count = lax.axis_size("dp"), lax.axis_size("seq")
+    pairs = []
+    for g in range(groups):
+        pairs += [(g * count + end, (g ^ 1) * count + end) for end in (0, count - 1)]
+        for i in range(1, count - 1, 2):
+            pairs += [(g * count + i, g * count + i + 1), (g * count + i + 1, g * count + i)]
+    return lax.ppermute(value, ("dp", "seq"), pairs)
 
 
 VMEM_SPEC = pl.BlockSpec(memory_space=pltpu.VMEM)
@@ -332,31 +350,34 @@
     return pl.CostEstimate(flops=flops, bytes_accessed=moved, transcendentals=0)
 
 
-def local(features, slot_kind, block_gain, block_shift, block_weight, block_bias, final_gain, final_shift,
-          latent_weight, latent_bias, embed_weight, embed_bias):
-    seq, dp = lax.axis_size("seq"), lax.axis_size("dp")
+def encode_buffers(cells, channels):
+    return [
+        pltpu.VMEM((3, cells, channels), BF16),
+        pltpu.VMEM((3, 2, cells // 2 + 2 * SLOT_COLS, channels), BF16),
+        pltpu.VMEM((cells, channels), BF16),
+    ]
+
+
+def encode_flops(cells, channels, lat):
+    return cells * channels * 2 * 9 * (channels + lat)
+
+
+def begin(features, slot_kind, block_weight, embed_weight, embed_bias, small):
     slots = slot_kind.shape[1]
     channels = features.shape[2]
     cells = SLOT_ROWS * SLOT_COLS
     tokens = cells // 4
     feats, width = embed_weight.shape
-    small = (block_gain, block_shift, block_bias, final_gain, final_shift, latent_weight.T, latent_bias)
-    offsets = tuple(range(2, seq // 2, 2))
-    others = [exchange(slot_kind, "seq", offset) for offset in offsets]
-    buffers = [
-        pltpu.VMEM((3, cells, channels), BF16),
-        pltpu.VMEM((3, 2, cells // 2 + 2 * SLOT_COLS, channels), BF16),
-        pltpu.VMEM((cells, channels), BF16),
-    ]
-    flops = cells * channels * 2 * 9 * (channels + latent_weight.shape[1] // 9)
-    state, x, w, perm, piece, last, *small = pl.pallas_call(
+    buffers = encode_buffers(cells, channels)
+    flops = encode_flops(cells, channels, small[6].shape[0])
+    return pl.pallas_call(
         begin_kernel,
         out_shape=[
             pltpu.SMEM((8,), jnp.int32),
             pltpu.VMEM((slots, cells, channels), BF16),
             pltpu.VMEM(block_weight.shape, BF16),
             pltpu.VMEM((cells, cells), BF16),
-            jax.ShapeDtypeStruct((feats + 16, width), BF16),
+            pltpu.VMEM((feats + 16, width), BF16),
             pltpu.VMEM((tokens, feats), BF16),
         ] + [pltpu.VMEM(v.shape, v.dtype) for v in small],
         in_specs=[ANY_SPEC] * (5 + len(small)),
@@ -375,6 +396,21 @@
         cost_estimate=cost(flops, block_weight.size * 2),
         name="begin",
     )(slot_kind, features, block_weight, embed_weight, embed_bias, *small)
+
+
+def local(features, slot_kind, block_gain, block_shift, block_weight, block_bias, final_gain, final_shift,
+          latent_weight, latent_bias, embed_weight, embed_bias):
+    seq, dp = lax.axis_size("seq"), lax.axis_size("dp")
+    channels = features.shape[2]
+    cells = SLOT_ROWS * SLOT_COLS
+    tokens = cells // 4
+    feats, width = embed_weight.shape
+    small = (block_gain, block_shift, block_bias, final_gain, final_shift, latent_weight.T, latent_bias)
+    offsets = tuple(range(2, seq // 2, 2))
+    others = [exchange(slot_kind, "seq", offset) for offset in offsets]
+    buffers = encode_buffers(cells, channels)
+    flops = encode_flops(cells, channels, latent_bias.shape[0])
+    state, x, w, perm, piece, last, *small = begin(features, slot_kind, block_weight, embed_weight, embed_bias, small)
     message, sums = pl.pallas_call(
         functools.partial(middle_kernel, offsets),
         out_shape=[jax.ShapeDtypeStruct((2 * tokens + 16, feats), BF16), pltpu.SMEM((1,), jnp.int32)],
@@ -387,7 +423,7 @@
         name="middle",
     )(state, x, w, perm, last, *small, *others)
     even = exchange(message, "seq", 1)
-    odd = swap_odd_pairs(message, "seq")
+    odd = swap_odd_pairs(message)
     pieces = [piece] + [exchange(piece, "dp", offset) for offset in range(1, dp)]
     third = pl.pallas_call(
         final_kernel,

time: 22.7 us -> 19.5 us (0.86)
  Pallas kernels: 13.5 us -> 9.4 us
  waiting for transfers between devices: 2.01 us -> 4.86 us
  starting transfers between devices: 6.98 us -> 5.07 us
    pallas_call x1, Pallas kernels: 2.8 us -> 0.01 us  [local(): pl.pallas_call(final_kernel, out_shape=pltpu.VMEM((tokens, feats), BF16),...]
    ppermute x5, waiting for transfers between devices: 0.01 us -> 2.47 us  [exchange(): return lax.ppermute(value, axis, [(i, i ^ offset) for i in range(count)])]
    ppermute x1, starting transfers between devices: 1.91 us -> 0.01 us  [swap_odd_pairs(): return lax.ppermute(value, ('dp', 'seq'), pairs)]
    pallas_call x1, Pallas kernels: 6.56 us -> 5.48 us  [begin(): pl.pallas_call(begin_kernel, out_shape=[pltpu.SMEM((8,), jnp.int32), pltp...]
    ppermute x1, waiting for transfers between devices: 2 us -> 2.39 us  [swap_odd_pairs(): return lax.ppermute(value, ('dp', 'seq'), pairs)]
  transfers between devices with their start and end apart: 6 -> 6, of which waited for: 1 -> 2; matrix products, arithmetic and copies ran while one was open for 0% -> 0% of each run, Pallas kernels for 55% -> 43%
where the time goes in v3:
time: 19.5 us; the launch traced here: 19.4 us
  Pallas kernels  9.4 us (48%)
  starting transfers between devices  5.07 us (26%)
  waiting for transfers between devices  4.86 us (25%)
    pallas_call x1, Pallas kernels, begin(): pl.pallas_call(begin_kernel, out_shape=[pltpu.SMEM((8,), jnp.int32), pltp...  5.48 us
    ppermute x5, starting transfers between devices, exchange(): return lax.ppermute(value, axis, [(i, i ^ offset) for i in range(count)])  5.06 us
    pallas_call x1, Pallas kernels, local(): pl.pallas_call(functools.partial(middle_kernel, offsets), out_shape=[jax....  2.83 us
    ppermute x5, waiting for transfers between devices, exchange(): return lax.ppermute(value, axis, [(i, i ^ offset) for i in range(count)])  2.47 us
    ppermute x1, waiting for transfers between devices, swap_odd_pairs(): return lax.ppermute(value, ('dp', 'seq'), pairs)  2.39 us
    pallas_call x1, Pallas kernels, local(): pl.pallas_call(functools.partial(join_kernel, dp), out_shape=jax.ShapeDty...  1.08 us
  transfers between devices with their start and end apart: 6, of which 2 were waited for; matrix products, arithmetic and copies ran while one was open for 0% of the time, Pallas kernels for 43%

profile of v3, /device:TPU:16, one launch (start us, length us, event | category | flops | bytes accessed | tf_op | source)
XLA Modules:
  0.0 19.4 jit_solution(15167273637117232977)
XLA Ops:
  0.0 1.6 %collective-permute-start = (s32[1,3]{1,0:T(1,128)}, s32[1,3]{1,0:T(1,128)S(1)}, u32[]{:S(2)}, u32[]{:S(2)}) collective-permute-start(s32[1,3]{1,0:T(1,128)} %kind_hbm.1), channel_id=1, source_target_pairs={{0,2},{1,3},{2,0},{3,1},{4,6},{5,7},{6,4},{7,5},{8,10},{9,11},{10,... | collective-permute-start | bytes 44 | tf_op jit(solution)/shard_map/ppermute | solution.py:330
  1.6 5.5 %begin.1 = (s32[8]{0:T(128)S(4)}, bf16[3,256,512]{2,1,0:T(8,128)(2,1)S(1)}, bf16[4608,512]{1,0:T(8,128)(2,1)S(1)}, bf16[256,256]{1,0:T(8,128)(2,1)S(1)}, bf16[80...) custom-call(s32[1,3]{1,0:T(1,128)} %kind_hbm.1, ...), custom_call_target="tpu_custom_call" | custom-call | flops 1245708288 | bytes 4718592 | tf_op jit(solution)/shard_map/begin/pallas_call | solution.py:373
  7.1 0.1 collective-permute-start.3
  7.1 1.6 %collective-permute-start.4 = (bf16[80,288]{1,0:T(8,128)(2,1)S(1)}, bf16[80,288]{1,0:T(8,128)(2,1)S(1)}, u32[]{:S(2)}, u32[]{:S(2)}) collective-permute-start(bf16[80,288]{1,0:T(8,128)(2,1)S(1)} %get-tuple-element.34.rest_0_), channel_id=1, source_target_pairs={{0,16},{8,24},{16,0},{24,8},{1,17},{9,25},{17,1},{25,9},{2,18},{10... | collective-permute-start | bytes 138248 | tf_op jit(solution)/shard_map/ppermute | solution.py:330
  8.7 0.3 %collective-permute-start.5 = (bf16[80,288]{1,0:T(8,128)(2,1)S(1)}, bf16[80,288]{1,0:T(8,128)(2,1)S(1)}, u32[]{:S(2)}, u32[]{:S(2)}) collective-permute-start(bf16[80,288]{1,0:T(8,128)(2,1)S(1)} %get-tuple-element.34.rest_0_), channel_id=1, source_target_pairs={{0,24},{8,16},{16,8},{24,0},{1,25},{9,17},{17,9},{25,1},{2,26},{10... | collective-permute-start | bytes 138248 | tf_op jit(solution)/shard_map/ppermute | solution.py:330
  9.0 0.0 collective-permute-done.rest_7_
  9.0 2.8 %middle.1 = (bf16[144,64]{1,0:T(8,128)(2,1)S(1)}, s32[1]{0:T(128)S(4)}) custom-call(s32[8]{0:T(128)S(4)} %get-tuple-element.20.state_ref, bf16[3,256,512]{2,1,0:T(8,128)(2,1)S(1)} %get-tuple-element.21.x_ref, bf16[4608,512]{1,0:T(8,128)(2,1)S(1)} %get-tuple-element.22.w_ref, bf16[256,256]{1,0:T(8,128)(2,1)S(1)} %get-tuple-element.23.perm_ref, ...), custom_call_target="tpu_custom_call" | custom-call | flops 1245708288 | bytes 4718592 | tf_op jit(solution)/shard_map/middle/pallas_call | solution.py:414
  11.9 1.6 %collective-permute-start.1 = (bf16[144,64]{1,0:T(8,128)(2,1)S(1)}, bf16[144,64]{1,0:T(8,128)(2,1)S(1)}, u32[]{:S(2)}, u32[]{:S(2)}) collective-permute-start(bf16[144,64]{1,0:T(8,128)(2,1)S(1)} %get-tuple-element.33.own_ref), channel_id=1, source_target_pairs={{0,1},{1,0},{2,3},{3,2},{4,5},{5,4},{6,7},{7,6},{8,9},{9,8},{10,11... | collective-permute-start | bytes 55304 | tf_op jit(solution)/shard_map/ppermute | solution.py:330
  13.4 0.0 collective-permute-start.2
  13.4 2.5 %collective-permute-done.1.even_ref = bf16[144,64]{1,0:T(8,128)(2,1)S(1)} collective-permute-done((bf16[144,64]{1,0:T(8,128)(2,1)S(1)}, bf16[144,64]{1,0:T(8,128)(2,1)S(1)}, u32[]{:S(2)}, u32[]{:S(2)}) %collective-permute-start.1) | collective-permute-done | bytes 18464 | tf_op jit(solution)/shard_map/ppermute | solution.py:330
  15.9 2.4 %collective-permute-done.2.odd_ref = bf16[144,64]{1,0:T(8,128)(2,1)S(1)} collective-permute-done((bf16[144,64]{1,0:T(8,128)(2,1)S(1)}, bf16[144,64]{1,0:T(8,128)(2,1)S(1)}, u32[]{:S(2)}, u32[]{:S(2)}) %collective-permute-start.2) | collective-permute-done | bytes 18464 | tf_op jit(solution)/shard_map/ppermute | solution.py:340
  18.3 0.0 collective-permute-done.3.rest_1_
  18.3 0.0 collective-permute-done.4.rest_2_
  18.3 0.0 collective-permute-done.5.rest_3_
  18.3 1.1 %join.1 = bf16[1,128,1152]{2,1,0:T(8,128)(2,1)} custom-call(s32[8]{0:T(128)S(4)} %get-tuple-element.20.state_ref, s32[1]{0:T(128)S(4)} %get-tuple-element.32.sums_ref, bf16[144,64]{1,0:T(8,128)(2,1)S(1)} %get-tuple-element.33.own_ref, bf16[64,64]{1,0:T(8,128)(2,1)S(1)} %final.1.third_ref, bf16[144,64]{1,0:T(8,128)(2,1)S(1)} %collective-permute-done.1.even_ref, ...), custom_call_target="tpu_custom_call" | custom-call | flops 18874368 | bytes 294912 | tf_op jit(solution)/shard_map/join/pallas_call | solution.py:438
  (1 shorter events, 0.0 us)
Async XLA Ops:
  0.0 9.0 %collective-permute-start = (s32[1,3]{1,0:T(1,128)}, s32[1,3]{1,0:T(1,128)S(1)}, u32[]{:S(2)}, u32[]{:S(2)}) collective-permute-start(s32[1,3]{1,0:T(1,128)} %kind_hbm.1), channel_id=1, source_target_pairs={{0,2},{1,3},{2,0},{3,1},{4,6},{5,7},{6,4},{7,5},{8,10},{9,11},{10,... | collective-permute-start | bytes 44 | tf_op jit(solution)/shard_map/ppermute | solution.py:330
  7.1 11.2 %collective-permute-start.3 = (bf16[80,288]{1,0:T(8,128)(2,1)S(1)}, bf16[80,288]{1,0:T(8,128)(2,1)S(1)}, u32[]{:S(2)}, u32[]{:S(2)}) collective-permute-start(bf16[80,288]{1,0:T(8,128)(2,1)S(1)} %get-tuple-element.34.rest_0_), channel_id=1, source_target_pairs={{0,8},{8,0},{16,24},{24,16},{1,9},{9,1},{17,25},{25,17},{2,10},{10... | collective-permute-start | bytes 138248 | tf_op jit(solution)/shard_map/ppermute | solution.py:330
  7.1 11.1 %collective-permute-start.4 = (bf16[80,288]{1,0:T(8,128)(2,1)S(1)}, bf16[80,288]{1,0:T(8,128)(2,1)S(1)}, u32[]{:S(2)}, u32[]{:S(2)}) collective-permute-start(bf16[80,288]{1,0:T(8,128)(2,1)S(1)} %get-tuple-element.34.rest_0_), channel_id=1, source_target_pairs={{0,16},{8,24},{16,0},{24,8},{1,17},{9,25},{17,1},{25,9},{2,18},{10... | collective-permute-start | bytes 138248 | tf_op jit(solution)/shard_map/ppermute | solution.py:330
  8.7 9.5 %collective-permute-start.5 = (bf16[80,288]{1,0:T(8,128)(2,1)S(1)}, bf16[80,288]{1,0:T(8,128)(2,1)S(1)}, u32[]{:S(2)}, u32[]{:S(2)}) collective-permute-start(bf16[80,288]{1,0:T(8,128)(2,1)S(1)} %get-tuple-element.34.rest_0_), channel_id=1, source_target_pairs={{0,24},{8,16},{16,8},{24,0},{1,25},{9,17},{17,9},{25,1},{2,26},{10... | collective-permute-start | bytes 138248 | tf_op jit(solution)/shard_map/ppermute | solution.py:330
  11.9 4.0 %collective-permute-start.1 = (bf16[144,64]{1,0:T(8,128)(2,1)S(1)}, bf16[144,64]{1,0:T(8,128)(2,1)S(1)}, u32[]{:S(2)}, u32[]{:S(2)}) collective-permute-start(bf16[144,64]{1,0:T(8,128)(2,1)S(1)} %get-tuple-element.33.own_ref), channel_id=1, source_target_pairs={{0,1},{1,0},{2,3},{3,2},{4,5},{5,4},{6,7},{7,6},{8,9},{9,8},{10,11... | collective-permute-start | bytes 55304 | tf_op jit(solution)/shard_map/ppermute | solution.py:330
  13.4 4.9 %collective-permute-start.2 = (bf16[144,64]{1,0:T(8,128)(2,1)S(1)}, bf16[144,64]{1,0:T(8,128)(2,1)S(1)}, u32[]{:S(2)}, u32[]{:S(2)}) collective-permute-start(bf16[144,64]{1,0:T(8,128)(2,1)S(1)} %get-tuple-element.33.own_ref), channel_id=1, source_target_pairs={{0,8},{7,15},{1,2},{2,1},{3,4},{4,3},{5,6},{6,5},{8,0},{15,7},{9,1... | collective-permute-start | bytes 55304 | tf_op jit(solution)/shard_map/ppermute | solution.py:340

commit v4 on v3

v4 whole, which is shorter than its diff:
```python
import functools
import jax
import jax.numpy as jnp
from jax import lax
from jax.sharding import PartitionSpec as P
from jax.sharding import PartitionSpec as P
from jax.experimental import pallas as pl
from jax.experimental.pallas import tpu as pltpu

GROUPS = 32
SLOT_ROWS = 32
SLOT_COLS = 8
LATENT_SHIFT = 0.0609
LATENT_SCALE = 1.5305
NORM_EPSILON = 1e-06
LANES = 128
ROW_STEPS = (0, -1, 1)
VMEM_BYTES = 64 * 1024 * 1024
F32 = jnp.float32
BF16 = jnp.bfloat16


def group_total(stats, same_group):
    rows, channels = stats.shape
    chunks = channels // LANES
    packed = jnp.concatenate([stats[:, k * LANES:(k + 1) * LANES] for k in range(chunks)], axis=0)
    high = packed.astype(BF16)
    rest = packed - high.astype(F32)
    middle = rest.astype(BF16)
    low = (rest - middle.astype(F32)).astype(BF16)
    total = sum(jnp.dot(piece, same_group, preferred_element_type=F32) for piece in (high, middle, low))
    return jnp.concatenate([total[k * rows:(k + 1) * rows] for k in range(chunks)], axis=1)


def affine(stats, joined, gain, shift, same_group, count):
    total = group_total(stats, same_group)
    mean, square = total[0:2] * (1.0 / count), total[2:4] * (1.0 / count)
    both_mean = 0.5 * (mean[0:1] + mean[1:2])
    both_square = 0.5 * (square[0:1] + square[1:2])
    mean = jnp.where(joined, both_mean, mean)
    square = jnp.where(joined, both_square, square)
    spread = jnp.maximum(square - mean * mean, 0.0)
    scale = lax.rsqrt(spread + NORM_EPSILON) * (0.5 * gain)
    return scale, 0.5 * shift - mean * scale


def half_stats(half):
    total = jnp.sum(half, axis=0, keepdims=True)
    return total, jnp.sum(half * half, axis=0, keepdims=True)


def norm_first_steps(x_ref, joined, gain, shift, same_group, z_ref, u_ref):
    cells, channels = x_ref.shape
    half = cells // 2
    rows = cells // SLOT_COLS
    chunks = channels // LANES
    count = half * (channels // GROUPS)
    keep = jnp.where(joined, 1.0, 0.0).astype(F32)
    column = lax.broadcasted_iota(jnp.int32, (1, SLOT_COLS, 1), 1)
    parts = []
    for k in range(chunks):
        x = x_ref[:, k * LANES:(k + 1) * LANES].astype(F32)
        t0, q0 = half_stats(x[:half])
        t1, q1 = half_stats(x[half:])
        parts.append(jnp.concatenate([t0, t1, q0, q1], axis=0))
        yield
    scale, offset = affine(jnp.concatenate(parts, axis=1), joined, gain, shift, same_group, count)
    zero = jnp.zeros((SLOT_COLS, LANES), F32)
    for k in range(chunks):
        lanes = slice(k * LANES, (k + 1) * LANES)
        x = x_ref[:, lanes].astype(F32)
        v = jnp.concatenate([x[:half] * scale[0:1, lanes] + offset[0:1, lanes],
                             x[half:] * scale[1:2, lanes] + offset[1:2, lanes]], axis=0)
        act = v + v * jnp.tanh(v)
        act3 = act.reshape(rows, SLOT_COLS, LANES)
        left = jnp.where(column == 0, 0.0, pltpu.roll(act3, 1, 1)).reshape(cells, LANES)
        right = jnp.where(column == SLOT_COLS - 1, 0.0, pltpu.roll(act3, SLOT_COLS - 1, 1)).reshape(cells, LANES)
        for b, value in enumerate((left, act, right)):
            z_ref[b, :, lanes] = value.astype(BF16)
            over = value[half:half + SLOT_COLS] * keep
            under = value[half - SLOT_COLS:half] * keep
            u_ref[b, 0, :, lanes] = jnp.concatenate([zero, value[:half], over], axis=0).astype(BF16)
            u_ref[b, 1, :, lanes] = jnp.concatenate([under, value[half:], zero], axis=0).astype(BF16)
        yield


def conv_steps(x_ref, bias, wbuf, wait_weights, z_ref, u_ref, y_ref):
    cells, channels = x_ref.shape
    half = cells // 2
    tile = channels // 2
    totals = [x_ref[:, k * tile:(k + 1) * tile].astype(F32) + bias[:, k * tile:(k + 1) * tile] for k in range(2)]
    for step, a in enumerate(ROW_STEPS):
        wait_weights(step)
        for b in range(3):
            if a == 0:
                lhs = z_ref[b]
            else:
                first = 0 if a < 0 else 2 * SLOT_COLS
                lhs = jnp.concatenate([u_ref[b, h, first:first + half, :] for h in range(2)], axis=0)
            base = (3 * (a + 1) + b) * channels
            for k in range(2):
                totals[k] = totals[k] + jnp.dot(lhs, wbuf[base:base + channels, k * tile:(k + 1) * tile],
                                                preferred_element_type=F32)
                yield
    for k in range(2):
        y_ref[:, k * tile:(k + 1) * tile] = totals[k].astype(BF16)
    yield


def drain(steps):
    for _ in steps:
        pass


def interleave(main, *others):
    for _ in main:
        for steps in others:
            next(steps, None)
    for steps in others:
        drain(steps)


def norm_second_steps(y_ref, joined, gain, shift, same_group):
    cells, channels = y_ref.shape
    half = cells // 2
    chunks = channels // LANES
    count = half * (channels // GROUPS)
    parts = []
    for k in range(chunks):
        lanes = slice(k * LANES, (k + 1) * LANES)
        inner = y_ref[:, lanes].astype(F32)
        t0, q0 = half_stats(inner[:half])
        t1, q1 = half_stats(inner[half:])
        parts.append(jnp.concatenate([t0, t1, q0, q1], axis=0))
        yield
    scale, offset = affine(jnp.concatenate(parts, axis=1), joined, gain, shift, same_group, count)
    for k in range(chunks):
        lanes = slice(k * LANES, (k + 1) * LANES)
        y = y_ref[:, lanes].astype(F32)
        v = jnp.concatenate([y[:half] * scale[0:1, lanes] + offset[0:1, lanes],
                             y[half:] * scale[1:2, lanes] + offset[1:2, lanes]], axis=0)
        y_ref[:, lanes] = (v + v * jnp.tanh(v)).astype(BF16)
        yield


def to_patches_steps(store, y_ref, joined, table_ref, bias, gather):
    cells, channels = y_ref.shape
    rows = cells // SLOT_COLS
    mid = rows // 2
    tokens = gather.shape[0]
    lat = channels // GROUPS
    keep = jnp.where(joined, 1.0, 0.0).astype(F32)
    column = lax.broadcasted_iota(jnp.int32, (1, SLOT_COLS, 1), 1)
    block = whole(lax.broadcasted_iota(jnp.int32, (1, SLOT_COLS, LANES), 2), lat)
    taps = jnp.dot(y_ref[...], table_ref[...], preferred_element_type=F32)
    yield
    from_left, here, from_right = (taps[:, k * LANES:(k + 1) * LANES].reshape(rows, SLOT_COLS, LANES) for k in range(3))
    moved = here + jnp.where(column == 0, 0.0, pltpu.roll(from_left, 1, 1))
    moved = moved + jnp.where(column == SLOT_COLS - 1, 0.0, pltpu.roll(from_right, SLOT_COLS - 1, 1))
    yield
    blank = jnp.zeros((1, SLOT_COLS, LANES), F32)
    above = jnp.concatenate([blank, moved[:mid - 1], moved[mid - 1:mid] * keep, moved[mid:rows - 1]], axis=0)
    below = jnp.concatenate([moved[1:mid], moved[mid:mid + 1] * keep, moved[mid + 1:], blank], axis=0)
    step_up = (block == 0) | (block == 3)
    step_none = (block == 1) | (block == 4)
    mixed = jnp.where(step_up, above, jnp.where(step_none, moved, below)).reshape(cells, LANES)
    yield
    latent = mixed + pltpu.roll(mixed, LANES - lat, 1) + pltpu.roll(mixed, LANES - 2 * lat, 1)
    latent = ((latent + bias) - LATENT_SHIFT) * LATENT_SCALE
    corner = block - part(lax.broadcasted_iota(jnp.int32, (1, SLOT_COLS, LANES), 1), 2)
    corner = jnp.concatenate([corner, corner - 2], axis=0)
    latent = latent.reshape(rows // 2, 2, SLOT_COLS, LANES)
    latent = jnp.where((corner == 0)[None], latent, 0.0).reshape(cells, LANES)
    yield
    store(jnp.dot(gather, latent.astype(BF16), preferred_element_type=F32)[:, :4 * lat].astype(BF16))
    yield


def patch_tables(lw_ref, bias_ref, table_ref, bias4_ref):
    lat = lw_ref.shape[0] // 9
    weight = lw_ref[...].astype(F32)
    blank = jnp.zeros((2 * lat, weight.shape[1]), F32)
    for b in range(3):
        blocks = [weight[(3 * a + b) * lat:(3 * a + b + 1) * lat] for a in range(3)]
        table_ref[:, b * LANES:(b + 1) * LANES] = jnp.concatenate(blocks * 2 + [blank], axis=0).T.astype(BF16)
    bias4_ref[...] = jnp.concatenate([bias_ref[...].reshape(1, lat)] * (LANES // lat), axis=1)


def whole(value, size):
    return value >> (size.bit_length() - 1)


def part(value, size):
    return value & (size - 1)


def group_table(channels):
    width = channels // GROUPS
    r = whole(lax.broadcasted_iota(jnp.int32, (LANES, LANES), 0), width)
    c = whole(lax.broadcasted_iota(jnp.int32, (LANES, LANES), 1), width)
    return jnp.where(r == c, 1.0, 0.0).astype(BF16)


def patch_table(cells):
    half_cols = SLOT_COLS // 2
    token = lax.broadcasted_iota(jnp.int32, (cells // 4, cells), 0)
    cell = lax.broadcasted_iota(jnp.int32, (cells // 4, cells), 1)
    own = whole(whole(cell, SLOT_COLS), 2) * half_cols + whole(part(cell, SLOT_COLS), 2)
    return jnp.where(own == token, 1.0, 0.0).astype(BF16)


def finish_steps(store, y_ref, joined, gain, shift, same_group, table_ref, bias4, gather):
    yield from norm_second_steps(y_ref, joined, gain, shift, same_group)
    yield from to_patches_steps(store, y_ref, joined, table_ref, bias4, gather)


FIRST = 1


def vector(ref):
    return ref[...].reshape(1, ref.shape[0])


def begin_kernel(kind_hbm, feat_hbm, bw_hbm, ew_hbm, eb_hbm, *rest):
    names = 7
    small_hbm, rest = rest[:names], rest[names:]
    state_ref, x_ref, w_ref, perm_ref, piece_ref, y_ref, z_ref, u_ref, *rest = rest
    small, rest = rest[:names - 2], rest[names - 2:]
    table_ref, bias4_ref, kind_ref, lw_ref, lb_ref, ew_ref, eb_ref, ksem, xsem, wsem, ssem = rest
    gain1, shift1, bias1 = small[:3]
    slots, cells, channels = x_ref.shape
    kcopy = pltpu.make_async_copy(kind_hbm, kind_ref, ksem)
    kcopy.start()
    xcopies = [pltpu.make_async_copy(feat_hbm.at[0, pl.ds(s * cells, cells), :], x_ref.at[s], xsem.at[s])
               for s in range(slots)]
    depth = 3 * channels
    wcopies = [pltpu.make_async_copy(
        bw_hbm.at[pl.ds((a + 1) * depth, depth), :], w_ref.at[pl.ds((a + 1) * depth, depth), :], wsem.at[i])
        for i, a in enumerate(ROW_STEPS)]
    scopies = [pltpu.make_async_copy(src, dst, ssem.at[i])
               for i, (src, dst) in enumerate(zip(small_hbm + (ew_hbm, eb_hbm), small + [lw_ref, lb_ref, ew_ref, eb_ref]))]
    others = [k for k in range(slots) if k != FIRST]
    for c in [xcopies[FIRST]] + scopies + [xcopies[k] for k in others]:
        c.start()
    for c in wcopies:
        c.start(priority=1)
    perm_ref[...] = patch_table(cells)
    same_group = group_table(channels)
    kcopy.wait()
    live = jnp.int32(0)
    for s in range(slots):
        live = live + jnp.where(kind_ref[0, s] > 0, 1, 0).astype(jnp.int32)
        state_ref[2 + s] = kind_ref[0, s]
    state_ref[0] = live
    state_ref[1] = jnp.where(live > 2, 2, 0)
    for c in scopies + [xcopies[FIRST]]:
        c.wait()
    feats = ew_ref.shape[0]
    piece_ref[0:feats, :] = ew_ref[...]
    piece_ref[feats:, :] = jnp.broadcast_to(vector(eb_ref), (piece_ref.shape[0] - feats, ew_ref.shape[1]))

    def first_norm(k):
        return norm_first_steps(x_ref.at[k], kind_ref[0, k] == 2, vector(gain1), vector(shift1), same_group,
                                z_ref.at[k], u_ref.at[k])

    def side_work():
        for k in others:
            yield from first_norm(k)
        patch_tables(lw_ref, lb_ref, table_ref, bias4_ref)
        yield

    drain(first_norm(FIRST))
    for k in others:
        xcopies[k].wait()
    interleave(conv_steps(x_ref.at[FIRST], vector(bias1), w_ref, lambda step: wcopies[step].wait(),
                          z_ref.at[FIRST], u_ref.at[FIRST], y_ref), side_work())


def second_norm(y_ref, kind, small):
    return norm_second_steps(y_ref, kind == 2, vector(small[3]), vector(small[4]), group_table(y_ref.shape[1]))


def patches(store, y_ref, kind, small, perm_ref):
    return to_patches_steps(store, y_ref, kind == 2, small[5], small[6][...], perm_ref[...])


def chain(*parts):
    for steps in parts:
        yield from steps


def count_live(kind_ref):
    total = jnp.int32(-2)
    for s in range(kind_ref.shape[1]):
        total = total + jnp.where(kind_ref[0, s] > 0, 1, 0).astype(jnp.int32)
    return total


def middle_kernel(offsets, state_ref, x_ref, w_ref, perm_ref, first_ref, z_ref, u_ref, *rest):
    names = 7
    small, rest = rest[:names], rest[names:]
    others, rest = rest[:len(offsets)], rest[len(offsets):]
    message_ref, sums_ref, *rest = rest
    early_ref, y_ref, *rest = rest
    kinds, ksem = rest[:-1], rest[-1]
    copies = [pltpu.make_async_copy(src, dst, ksem.at[i]) for i, (src, dst) in enumerate(zip(others, kinds))]
    for c in copies:
        c.start()
    tokens = first_ref.shape[0] // 4
    feats = message_ref.shape[1]
    slot = state_ref[1]
    early_ref[...] = first_ref[...]
    first_at = jnp.where(state_ref[0] == 2, 0, tokens)

    def store_at(row):
        def store(value):
            message_ref[pl.ds(pl.multiple_of(row, tokens), tokens), :] = value
        return store

    kind, early_kind = state_ref[2 + slot], state_ref[2 + FIRST]
    interleave(conv_steps(x_ref.at[slot], vector(small[2]), w_ref, lambda step: None, z_ref.at[slot], u_ref.at[slot],
                          y_ref), second_norm(early_ref, early_kind, small))
    interleave(chain(second_norm(y_ref, kind, small), patches(store_at(tokens - first_at), y_ref, kind, small, perm_ref)),
               patches(store_at(first_at), early_ref, early_kind, small, perm_ref))
    for c in copies:
        c.wait()
    position = lax.axis_index("seq")
    mine = state_ref[0] - 2
    below, above = jnp.int32(0), mine
    for offset, kind_ref in zip(offsets, kinds):
        other = count_live(kind_ref)
        lower = (position ^ offset) < position
        below = below + jnp.where(lower, other, 0)
        above = above + jnp.where(lower, 0, other)
    first_half = position < lax.axis_size("seq") // 2
    passed = jnp.where(position % 2 == 0, mine, 0)
    sums_ref[0] = jnp.where(first_half, below, -above)
    told = jnp.where(first_half, below + passed, passed - above)
    message_ref[2 * tokens:, :] = jnp.full((message_ref.shape[0] - 2 * tokens, feats), told.astype(F32)).astype(BF16)


def final_kernel(state_ref, x_ref, w_ref, perm_ref, z_ref, u_ref, *rest):
    small, rest = rest[:7], rest[7:]
    out_ref, y_ref = rest

    @pl.when(state_ref[0] > 2)
    def _():
        def store(value):
            out_ref[...] = value

        drain(conv_steps(x_ref.at[0], vector(small[2]), w_ref, lambda step: None, z_ref.at[0], u_ref.at[0], y_ref))
        drain(second_norm(y_ref, state_ref[2], small))
        drain(patches(store, y_ref, state_ref[2], small, perm_ref))

    @pl.when(state_ref[0] <= 2)
    def _():
        out_ref[...] = jnp.zeros_like(out_ref)


def join_kernel(parts, state_ref, sums_ref, own_ref, third_ref, even_ref, odd_ref, *rest):
    pieces, out_ref, embed_ref, source_ref = rest[:parts], *rest[parts:]
    live = state_ref[0]
    group, position = lax.axis_index("dp"), lax.axis_index("seq")
    odd = position % 2
    tokens, feats = third_ref.shape
    width = pieces[0].shape[1]
    told = even_ref[2 * tokens:, :].astype(F32)[0, 0].astype(jnp.int32)
    carry = sums_ref[0] + told
    for j in range(parts):
        value = pieces[0][...]
        for k in range(1, parts):
            value = jnp.where((group ^ j) == k, pieces[k][...], value)
        embed_ref[:, j * width:(j + 1) * width] = value
    for k, ref in enumerate((even_ref, odd_ref, own_ref)):
        source_ref[2 * k] = ref[0:tokens, :]
        source_ref[2 * k + 1] = ref[tokens:2 * tokens, :]
    source_ref[6] = third_ref[...]
    weight = embed_ref[0:feats, :]
    bias = embed_ref[feats:feats + 1, :].astype(F32)
    for i in range(2):
        incoming = (1 - odd) * 2 + carry - 1 - i
        kept = 4 + live - 1 - (i - carry)
        patch = source_ref[jnp.clip(jnp.where(i < carry, incoming, kept), 0, 6)]
        value = jnp.dot(patch, weight, preferred_element_type=F32) + bias
        out_ref[0, i * tokens:(i + 1) * tokens, :] = value.astype(BF16)


def exchange(value, axis, offset):
    count = lax.axis_size(axis)
    return lax.ppermute(value, axis, [(i, i ^ offset) for i in range(count)])


def swap_odd_pairs(value):
    groups, count = lax.axis_size("dp"), lax.axis_size("seq")
    pairs = []
    for g in range(groups):
        pairs += [(g * count + end, (g ^ 1) * count + end) for end in (0, count - 1)]
        for i in range(1, count - 1, 2):
            pairs += [(g * count + i, g * count + i + 1), (g * count + i + 1, g * count + i)]
    return lax.ppermute(value, ("dp", "seq"), pairs)


VMEM_SPEC = pl.BlockSpec(memory_space=pltpu.VMEM)
SMEM_SPEC = pl.BlockSpec(memory_space=pltpu.SMEM)
ANY_SPEC = pl.BlockSpec(memory_space=pl.ANY)
MIB = 1024 * 1024


def cost(flops, moved):
    return pl.CostEstimate(flops=flops, bytes_accessed=moved, transcendentals=0)


def encode_flops(cells, channels, lat):
    return cells * channels * 2 * 9 * (channels + lat)


def begin(features, slot_kind, block_weight, embed_weight, embed_bias, small):
    slots = slot_kind.shape[1]
    channels = features.shape[2]
    cells = SLOT_ROWS * SLOT_COLS
    feats, width = embed_weight.shape
    flops = encode_flops(cells, channels, small[6].shape[0])
    return pl.pallas_call(
        begin_kernel,
        out_shape=[
            pltpu.SMEM((8,), jnp.int32),
            pltpu.VMEM((slots, cells, channels), BF16),
            pltpu.VMEM(block_weight.shape, BF16),
            pltpu.VMEM((cells // 4, cells), BF16),
            pltpu.VMEM((feats + 16, width), BF16),
            pltpu.VMEM((cells, channels), BF16),
            pltpu.VMEM((slots, 3, cells, channels), BF16),
            pltpu.VMEM((slots, 3, 2, cells // 2 + 2 * SLOT_COLS, channels), BF16),
        ] + [pltpu.VMEM(v.shape, v.dtype) for v in small[:5]]
        + [pltpu.VMEM((channels, 3 * LANES), BF16), pltpu.VMEM((1, LANES), F32)],
        in_specs=[ANY_SPEC] * (5 + len(small)),
        out_specs=[SMEM_SPEC] + [VMEM_SPEC] * (7 + len(small)),
        scratch_shapes=[
            pltpu.SMEM(slot_kind.shape, jnp.int32),
            pltpu.VMEM(small[5].shape, BF16),
            pltpu.VMEM(small[6].shape, F32),
            pltpu.VMEM(embed_weight.shape, BF16),
            pltpu.VMEM(embed_bias.shape, BF16),
            pltpu.SemaphoreType.DMA,
            pltpu.SemaphoreType.DMA((slots,)),
            pltpu.SemaphoreType.DMA((3,)),
            pltpu.SemaphoreType.DMA((len(small) + 2,)),
        ],
        compiler_params=pltpu.CompilerParams(vmem_limit_bytes=50 * MIB),
        cost_estimate=cost(flops, block_weight.size * 2),
        name="begin",
    )(slot_kind, features, block_weight, embed_weight, embed_bias, *small)


def local(features, slot_kind, block_gain, block_shift, block_weight, block_bias, final_gain, final_shift,
          latent_weight, latent_bias, embed_weight, embed_bias):
    seq, dp = lax.axis_size("seq"), lax.axis_size("dp")
    channels = features.shape[2]
    cells = SLOT_ROWS * SLOT_COLS
    tokens = cells // 4
    feats, width = embed_weight.shape
    small = (block_gain, block_shift, block_bias, final_gain, final_shift, latent_weight.T, latent_bias)
    offsets = tuple(range(2, seq // 2, 2))
    others = [exchange(slot_kind, "seq", offset) for offset in offsets]
    slot_buffer = pltpu.VMEM((cells, channels), BF16)
    flops = encode_flops(cells, channels, latent_bias.shape[0])
    state, x, w, perm, piece, first, z, u, *small = begin(features, slot_kind, block_weight, embed_weight, embed_bias, small)
    message, sums = pl.pallas_call(
        functools.partial(middle_kernel, offsets),
        out_shape=[jax.ShapeDtypeStruct((2 * tokens + 16, feats), BF16), pltpu.SMEM((1,), jnp.int32)],
        in_specs=[SMEM_SPEC] + [VMEM_SPEC] * (6 + len(small)) + [ANY_SPEC] * len(others),
        out_specs=[VMEM_SPEC, SMEM_SPEC],
        scratch_shapes=[slot_buffer] * 2 + [pltpu.SMEM(slot_kind.shape, jnp.int32) for _ in others]
        + [pltpu.SemaphoreType.DMA((len(others),))],
        compiler_params=pltpu.CompilerParams(vmem_limit_bytes=16 * MIB),
        cost_estimate=cost(flops, block_weight.size * 2),
        name="middle",
    )(state, x, w, perm, first, z, u, *small, *others)
    even = exchange(message, "seq", 1)
    odd = swap_odd_pairs(message)
    pieces = [piece] + [exchange(piece, "dp", offset) for offset in range(1, dp)]
    third = pl.pallas_call(
        final_kernel,
        out_shape=pltpu.VMEM((tokens, feats), BF16),
        in_specs=[SMEM_SPEC] + [VMEM_SPEC] * (5 + len(small)),
        out_specs=VMEM_SPEC,
        scratch_shapes=[slot_buffer],
        compiler_params=pltpu.CompilerParams(vmem_limit_bytes=16 * MIB),
        cost_estimate=cost(flops, block_weight.size * 2),
        name="final",
    )(state, x, w, perm, z, u, *small)
    return pl.pallas_call(
        functools.partial(join_kernel, dp),
        out_shape=jax.ShapeDtypeStruct((1, 2 * tokens, dp * width), BF16),
        in_specs=[SMEM_SPEC] * 2 + [VMEM_SPEC] * (4 + dp),
        out_specs=VMEM_SPEC,
        scratch_shapes=[pltpu.VMEM((feats + 16, dp * width), BF16), pltpu.VMEM((7, tokens, feats), BF16)],
        compiler_params=pltpu.CompilerParams(vmem_limit_bytes=8 * MIB),
        cost_estimate=cost(4 * tokens * feats * dp * width, 4 * tokens * dp * width),
        name="join",
    )(state, sums, message, third, even, odd, *pieces)


def solution(mesh):
    in_specs = (P("dp", "seq", None), P("dp", "seq")) + (P(),) * 8 + (P(None, "dp"), P("dp"))
    return jax.shard_map(local, mesh=mesh, in_specs=in_specs, out_specs=P("dp", "seq", None), check_vma=False)
```

time: 19.5 us -> 17 us (0.87)
  the two profiles are of different devices: /device:TPU:16 before, /device:TPU:0 now
where the time goes in v4:
time: 17 us; the launch traced here: 16.9 us
  Pallas kernels  7.64 us (45%)
  starting transfers between devices  6.7 us (39%)
  waiting for transfers between devices  2.52 us (15%)
    ppermute x5, starting transfers between devices, exchange(): return lax.ppermute(value, axis, [(i, i ^ offset) for i in range(count)])  6.39 us
    pallas_call x1, Pallas kernels, begin(): pl.pallas_call(begin_kernel, out_shape=[pltpu.SMEM((8,), jnp.int32), pltp...  4.23 us
    ppermute x5, waiting for transfers between devices, exchange(): return lax.ppermute(value, axis, [(i, i ^ offset) for i in range(count)])  2.52 us
    pallas_call x1, Pallas kernels, local(): pl.pallas_call(functools.partial(middle_kernel, offsets), out_shape=[jax....  2.33 us
    pallas_call x1, Pallas kernels, local(): pl.pallas_call(functools.partial(join_kernel, dp), out_shape=jax.ShapeDty...  1.08 us
  transfers between devices with their start and end apart: 6, of which 1 were waited for; matrix products, arithmetic and copies ran while one was open for 0% of the time, Pallas kernels for 39%

profile of v4, /device:TPU:0, one launch (start us, length us, event | category | flops | bytes accessed | tf_op | source)
XLA Modules:
  0.0 16.9 jit_solution(9882883233956533089)
XLA Ops:
  0.0 3.0 %collective-permute-start = (s32[1,3]{1,0:T(1,128)}, s32[1,3]{1,0:T(1,128)S(1)}, u32[]{:S(2)}, u32[]{:S(2)}) collective-permute-start(s32[1,3]{1,0:T(1,128)} %kind_hbm.1), channel_id=1, source_target_pairs={{0,2},{1,3},{2,0},{3,1},{4,6},{5,7},{6,4},{7,5},{8,10},{9,11},{10,... | collective-permute-start | bytes 44 | tf_op jit(solution)/shard_map/ppermute | solution.py:390
  3.0 4.2 %begin.1 = (s32[8]{0:T(128)S(4)}, bf16[3,256,512]{2,1,0:T(8,128)(2,1)S(1)}, bf16[4608,512]{1,0:T(8,128)(2,1)S(1)}, bf16[64,256]{1,0:T(8,128)(2,1)S(1)}, bf16[80,...) custom-call(s32[1,3]{1,0:T(1,128)} %kind_hbm.1, ...), custom_call_target="tpu_custom_call" | custom-call | flops 1245708288 | bytes 4718592 | tf_op jit(solution)/shard_map/begin/pallas_call | solution.py:423
  7.3 0.7 %collective-permute-start.5 = (bf16[80,288]{1,0:T(8,128)(2,1)S(1)}, bf16[80,288]{1,0:T(8,128)(2,1)S(1)}, u32[]{:S(2)}, u32[]{:S(2)}) collective-permute-start(bf16[80,288]{1,0:T(8,128)(2,1)S(1)} %get-tuple-element.38.rest_0_), channel_id=1, source_target_pairs={{0,24},{8,16},{16,8},{24,0},{1,25},{9,17},{17,9},{25,1},{2,26},{10... | collective-permute-start | bytes 138248 | tf_op jit(solution)/shard_map/ppermute | solution.py:390
  8.0 0.9 %collective-permute-start.4 = (bf16[80,288]{1,0:T(8,128)(2,1)S(1)}, bf16[80,288]{1,0:T(8,128)(2,1)S(1)}, u32[]{:S(2)}, u32[]{:S(2)}) collective-permute-start(bf16[80,288]{1,0:T(8,128)(2,1)S(1)} %get-tuple-element.38.rest_0_), channel_id=1, source_target_pairs={{0,16},{8,24},{16,0},{24,8},{1,17},{9,25},{17,1},{25,9},{2,18},{10... | collective-permute-start | bytes 138248 | tf_op jit(solution)/shard_map/ppermute | solution.py:390
  8.9 0.3 %collective-permute-start.3 = (bf16[80,288]{1,0:T(8,128)(2,1)S(1)}, bf16[80,288]{1,0:T(8,128)(2,1)S(1)}, u32[]{:S(2)}, u32[]{:S(2)}) collective-permute-start(bf16[80,288]{1,0:T(8,128)(2,1)S(1)} %get-tuple-element.38.rest_0_), channel_id=1, source_target_pairs={{0,8},{8,0},{16,24},{24,16},{1,9},{9,1},{17,25},{25,17},{2,10},{10... | collective-permute-start | bytes 138248 | tf_op jit(solution)/shard_map/ppermute | solution.py:390
  9.2 0.0 collective-permute-done.rest_7_
  9.2 2.3 %middle.1 = (bf16[144,64]{1,0:T(8,128)(2,1)S(1)}, s32[1]{0:T(128)S(4)}) custom-call(s32[8]{0:T(128)S(4)} %get-tuple-element.22.state_ref, bf16[3,256,512]{2,1,0:T(8,128)(2,1)S(1)} %get-tuple-element.23.x_ref, bf16[4608,512]{1,0:T(8,128)(2,1)S(1)} %get-tuple-element.24.w_ref, bf16[64,256]{1,0:T(8,128)(2,1)S(1)} %get-tuple-element.25.perm_ref, ...), custom_call_target="tpu_custom_call" | custom-call | flops 1245708288 | bytes 4718592 | tf_op jit(solution)/shard_map/middle/pallas_call | solution.py:468
  11.5 0.3 %collective-permute-start.2 = (bf16[144,64]{1,0:T(8,128)(2,1)S(1)}, bf16[144,64]{1,0:T(8,128)(2,1)S(1)}, u32[]{:S(2)}, u32[]{:S(2)}) collective-permute-start(bf16[144,64]{1,0:T(8,128)(2,1)S(1)} %get-tuple-element.37.own_ref), channel_id=1, source_target_pairs={{0,8},{7,15},{1,2},{2,1},{3,4},{4,3},{5,6},{6,5},{8,0},{15,7},{9,1... | collective-permute-start | bytes 55304 | tf_op jit(solution)/shard_map/ppermute | solution.py:400
  11.8 1.4 %collective-permute-start.1 = (bf16[144,64]{1,0:T(8,128)(2,1)S(1)}, bf16[144,64]{1,0:T(8,128)(2,1)S(1)}, u32[]{:S(2)}, u32[]{:S(2)}) collective-permute-start(bf16[144,64]{1,0:T(8,128)(2,1)S(1)} %get-tuple-element.37.own_ref), channel_id=1, source_target_pairs={{0,1},{1,0},{2,3},{3,2},{4,5},{5,4},{6,7},{7,6},{8,9},{9,8},{10,11... | collective-permute-start | bytes 55304 | tf_op jit(solution)/shard_map/ppermute | solution.py:390
  13.3 0.0 collective-permute-done.2.odd_ref
  13.3 2.5 %collective-permute-done.1.even_ref = bf16[144,64]{1,0:T(8,128)(2,1)S(1)} collective-permute-done((bf16[144,64]{1,0:T(8,128)(2,1)S(1)}, bf16[144,64]{1,0:T(8,128)(2,1)S(1)}, u32[]{:S(2)}, u32[]{:S(2)}) %collective-permute-start.1) | collective-permute-done | bytes 18464 | tf_op jit(solution)/shard_map/ppermute | solution.py:390
  15.8 0.0 collective-permute-done.5.rest_3_
  15.8 0.0 collective-permute-done.4.rest_2_
  15.8 0.0 collective-permute-done.3.rest_1_
  15.8 1.1 %join.1 = bf16[1,128,1152]{2,1,0:T(8,128)(2,1)} custom-call(s32[8]{0:T(128)S(4)} %get-tuple-element.22.state_ref, s32[1]{0:T(128)S(4)} %get-tuple-element.36.sums_ref, bf16[144,64]{1,0:T(8,128)(2,1)S(1)} %get-tuple-element.37.own_ref, bf16[64,64]{1,0:T(8,128)(2,1)S(1)} %final.1.third_ref, bf16[144,64]{1,0:T(8,128)(2,1)S(1)} %collective-permute-done.1.even_ref, ...), custom_call_target="tpu_custom_call" | custom-call | flops 18874368 | bytes 294912 | tf_op jit(solution)/shard_map/join/pallas_call | solution.py:492
  (1 shorter events, 0.0 us)
Async XLA Ops:
  0.0 9.2 %collective-permute-start = (s32[1,3]{1,0:T(1,128)}, s32[1,3]{1,0:T(1,128)S(1)}, u32[]{:S(2)}, u32[]{:S(2)}) collective-permute-start(s32[1,3]{1,0:T(1,128)} %kind_hbm.1), channel_id=1, source_target_pairs={{0,2},{1,3},{2,0},{3,1},{4,6},{5,7},{6,4},{7,5},{8,10},{9,11},{10,... | collective-permute-start | bytes 44 | tf_op jit(solution)/shard_map/ppermute | solution.py:390
  7.3 8.5 %collective-permute-start.5 = (bf16[80,288]{1,0:T(8,128)(2,1)S(1)}, bf16[80,288]{1,0:T(8,128)(2,1)S(1)}, u32[]{:S(2)}, u32[]{:S(2)}) collective-permute-start(bf16[80,288]{1,0:T(8,128)(2,1)S(1)} %get-tuple-element.38.rest_0_), channel_id=1, source_target_pairs={{0,24},{8,16},{16,8},{24,0},{1,25},{9,17},{17,9},{25,1},{2,26},{10... | collective-permute-start | bytes 138248 | tf_op jit(solution)/shard_map/ppermute | solution.py:390
  8.0 7.8 %collective-permute-start.4 = (bf16[80,288]{1,0:T(8,128)(2,1)S(1)}, bf16[80,288]{1,0:T(8,128)(2,1)S(1)}, u32[]{:S(2)}, u32[]{:S(2)}) collective-permute-start(bf16[80,288]{1,0:T(8,128)(2,1)S(1)} %get-tuple-element.38.rest_0_), channel_id=1, source_target_pairs={{0,16},{8,24},{16,0},{24,8},{1,17},{9,25},{17,1},{25,9},{2,18},{10... | collective-permute-start | bytes 138248 | tf_op jit(solution)/shard_map/ppermute | solution.py:390
  8.9 6.9 %collective-permute-start.3 = (bf16[80,288]{1,0:T(8,128)(2,1)S(1)}, bf16[80,288]{1,0:T(8,128)(2,1)S(1)}, u32[]{:S(2)}, u32[]{:S(2)}) collective-permute-start(bf16[80,288]{1,0:T(8,128)(2,1)S(1)} %get-tuple-element.38.rest_0_), channel_id=1, source_target_pairs={{0,8},{8,0},{16,24},{24,16},{1,9},{9,1},{17,25},{25,17},{2,10},{10... | collective-permute-start | bytes 138248 | tf_op jit(solution)/shard_map/ppermute | solution.py:390
  11.5 1.8 %collective-permute-start.2 = (bf16[144,64]{1,0:T(8,128)(2,1)S(1)}, bf16[144,64]{1,0:T(8,128)(2,1)S(1)}, u32[]{:S(2)}, u32[]{:S(2)}) collective-permute-start(bf16[144,64]{1,0:T(8,128)(2,1)S(1)} %get-tuple-element.37.own_ref), channel_id=1, source_target_pairs={{0,8},{7,15},{1,2},{2,1},{3,4},{4,3},{5,6},{6,5},{8,0},{15,7},{9,1... | collective-permute-start | bytes 55304 | tf_op jit(solution)/shard_map/ppermute | solution.py:400
  11.8 4.0 %collective-permute-start.1 = (bf16[144,64]{1,0:T(8,128)(2,1)S(1)}, bf16[144,64]{1,0:T(8,128)(2,1)S(1)}, u32[]{:S(2)}, u32[]{:S(2)}) collective-permute-start(bf16[144,64]{1,0:T(8,128)(2,1)S(1)} %get-tuple-element.37.own_ref), channel_id=1, source_target_pairs={{0,1},{1,0},{2,3},{3,2},{4,5},{5,4},{6,7},{7,6},{8,9},{9,8},{10,11... | collective-permute-start | bytes 55304 | tf_op jit(solution)/shard_map/ppermute | solution.py:390

commit v5 on v4

--- a/solution.py
+++ b/solution.py
@@ -307,21 +307,25 @@
     for c in copies:
         c.start()
     tokens = first_ref.shape[0] // 4
-    feats = message_ref.shape[1]
+    feats = message_ref.shape[1] // 2
     slot = state_ref[1]
     early_ref[...] = first_ref[...]
-    first_at = jnp.where(state_ref[0] == 2, 0, tokens)
-
-    def store_at(row):
+    found = {}
+
+    def keep_as(name):
         def store(value):
-            message_ref[pl.ds(pl.multiple_of(row, tokens), tokens), :] = value
+            found[name] = value
         return store
 
     kind, early_kind = state_ref[2 + slot], state_ref[2 + FIRST]
     interleave(conv_steps(x_ref.at[slot], vector(small[2]), w_ref, lambda step: None, z_ref.at[slot], u_ref.at[slot],
                           y_ref), second_norm(early_ref, early_kind, small))
-    interleave(chain(second_norm(y_ref, kind, small), patches(store_at(tokens - first_at), y_ref, kind, small, perm_ref)),
-               patches(store_at(first_at), early_ref, early_kind, small, perm_ref))
+    interleave(chain(second_norm(y_ref, kind, small), patches(keep_as("second"), y_ref, kind, small, perm_ref)),
+               patches(keep_as("first"), early_ref, early_kind, small, perm_ref))
+    first_is_last = state_ref[0] == 2
+    last = jnp.where(first_is_last, found["first"], found["second"])
+    before = jnp.where(first_is_last, found["second"], found["first"])
+    message_ref[0:tokens, :] = jnp.concatenate([last, before], axis=1)
     for c in copies:
         c.wait()
     position = lax.axis_index("seq")
@@ -336,53 +340,63 @@
     passed = jnp.where(position % 2 == 0, mine, 0)
     sums_ref[0] = jnp.where(first_half, below, -above)
     told = jnp.where(first_half, below + passed, passed - above)
-    message_ref[2 * tokens:, :] = jnp.full((message_ref.shape[0] - 2 * tokens, feats), told.astype(F32)).astype(BF16)
-
-
-def final_kernel(state_ref, x_ref, w_ref, perm_ref, z_ref, u_ref, *rest):
-    small, rest = rest[:7], rest[7:]
-    out_ref, y_ref = rest
+    message_ref[tokens:, :] = jnp.full((message_ref.shape[0] - tokens, 2 * feats), told.astype(F32)).astype(BF16)
+
+
+def final_kernel(parts, state_ref, x_ref, w_ref, perm_ref, z_ref, u_ref, *rest):
+    pieces, small, rest = rest[:parts], rest[parts:parts + 7], rest[parts + 7:]
+    out_ref, embed_ref, y_ref = rest
+    group = lax.axis_index("dp")
+    width = pieces[0].shape[1]
+
+    def lay_out():
+        for j in range(parts):
+            value = pieces[0][...]
+            for k in range(1, parts):
+                value = jnp.where((group ^ j) == k, pieces[k][...], value)
+            embed_ref[:, j * width:(j + 1) * width] = value
+            yield
 
     @pl.when(state_ref[0] > 2)
     def _():
         def store(value):
             out_ref[...] = value
 
-        drain(conv_steps(x_ref.at[0], vector(small[2]), w_ref, lambda step: None, z_ref.at[0], u_ref.at[0], y_ref))
+        interleave(conv_steps(x_ref.at[0], vector(small[2]), w_ref, lambda step: None, z_ref.at[0], u_ref.at[0], y_ref),
+                   lay_out())
         drain(second_norm(y_ref, state_ref[2], small))
         drain(patches(store, y_ref, state_ref[2], small, perm_ref))
 
     @pl.when(state_ref[0] <= 2)
     def _():
+        drain(lay_out())
         out_ref[...] = jnp.zeros_like(out_ref)
 
 
-def join_kernel(parts, state_ref, sums_ref, own_ref, third_ref, even_ref, odd_ref, *rest):
-    pieces, out_ref, embed_ref, source_ref = rest[:parts], *rest[parts:]
+def join_kernel(state_ref, sums_ref, own_ref, third_ref, odd_ref, even_ref, embed_ref, out_ref, source_ref, value_ref, sem):
     live = state_ref[0]
-    group, position = lax.axis_index("dp"), lax.axis_index("seq")
-    odd = position % 2
+    odd = lax.axis_index("seq") % 2
     tokens, feats = third_ref.shape
-    width = pieces[0].shape[1]
-    told = even_ref[2 * tokens:, :].astype(F32)[0, 0].astype(jnp.int32)
+    told = even_ref[tokens:, :].astype(F32)[0, 0].astype(jnp.int32)
     carry = sums_ref[0] + told
-    for j in range(parts):
-        value = pieces[0][...]
-        for k in range(1, parts):
-            value = jnp.where((group ^ j) == k, pieces[k][...], value)
-        embed_ref[:, j * width:(j + 1) * width] = value
     for k, ref in enumerate((even_ref, odd_ref, own_ref)):
-        source_ref[2 * k] = ref[0:tokens, :]
-        source_ref[2 * k + 1] = ref[tokens:2 * tokens, :]
+        source_ref[2 * k] = ref[0:tokens, 0:feats]
+        source_ref[2 * k + 1] = ref[0:tokens, feats:]
     source_ref[6] = third_ref[...]
     weight = embed_ref[0:feats, :]
     bias = embed_ref[feats:feats + 1, :].astype(F32)
+    copies = []
     for i in range(2):
         incoming = (1 - odd) * 2 + carry - 1 - i
         kept = 4 + live - 1 - (i - carry)
         patch = source_ref[jnp.clip(jnp.where(i < carry, incoming, kept), 0, 6)]
         value = jnp.dot(patch, weight, preferred_element_type=F32) + bias
-        out_ref[0, i * tokens:(i + 1) * tokens, :] = value.astype(BF16)
+        rows = pl.ds(i * tokens, tokens)
+        value_ref[rows, :] = value.astype(BF16)
+        copies.append(pltpu.make_async_copy(value_ref.at[rows, :], out_ref.at[0, rows, :], sem.at[i]))
+        copies[i].start()
+    for c in copies:
+        c.wait()
 
 
 def exchange(value, axis, offset):
@@ -467,7 +481,7 @@
     state, x, w, perm, piece, first, z, u, *small = begin(features, slot_kind, block_weight, embed_weight, embed_bias, small)
     message, sums = pl.pallas_call(
         functools.partial(middle_kernel, offsets),
-        out_shape=[jax.ShapeDtypeStruct((2 * tokens + 16, feats), BF16), pltpu.SMEM((1,), jnp.int32)],
+        out_shape=[jax.ShapeDtypeStruct((tokens + 16, 2 * feats), BF16), pltpu.SMEM((1,), jnp.int32)],
         in_specs=[SMEM_SPEC] + [VMEM_SPEC] * (6 + len(small)) + [ANY_SPEC] * len(others),
         out_specs=[VMEM_SPEC, SMEM_SPEC],
         scratch_shapes=[slot_buffer] * 2 + [pltpu.SMEM(slot_kind.shape, jnp.int32) for _ in others]
@@ -479,26 +493,27 @@
     even = exchange(message, "seq", 1)
     odd = swap_odd_pairs(message)
     pieces = [piece] + [exchange(piece, "dp", offset) for offset in range(1, dp)]
-    third = pl.pallas_call(
-        final_kernel,
-        out_shape=pltpu.VMEM((tokens, feats), BF16),
-        in_specs=[SMEM_SPEC] + [VMEM_SPEC] * (5 + len(small)),
-        out_specs=VMEM_SPEC,
+    third, embed = pl.pallas_call(
+        functools.partial(final_kernel, dp),
+        out_shape=[pltpu.VMEM((tokens, feats), BF16), pltpu.VMEM((feats + 16, dp * width), BF16)],
+        in_specs=[SMEM_SPEC] + [VMEM_SPEC] * (5 + dp + len(small)),
+        out_specs=[VMEM_SPEC] * 2,
         scratch_shapes=[slot_buffer],
         compiler_params=pltpu.CompilerParams(vmem_limit_bytes=16 * MIB),
         cost_estimate=cost(flops, block_weight.size * 2),
         name="final",
-    )(state, x, w, perm, z, u, *small)
+    )(state, x, w, perm, z, u, *pieces, *small)
     return pl.pallas_call(
-        functools.partial(join_kernel, dp),
+        join_kernel,
         out_shape=jax.ShapeDtypeStruct((1, 2 * tokens, dp * width), BF16),
-        in_specs=[SMEM_SPEC] * 2 + [VMEM_SPEC] * (4 + dp),
-        out_specs=VMEM_SPEC,
-        scratch_shapes=[pltpu.VMEM((feats + 16, dp * width), BF16), pltpu.VMEM((7, tokens, feats), BF16)],
+        in_specs=[SMEM_SPEC] * 2 + [VMEM_SPEC] * 5,
+        out_specs=ANY_SPEC,
+        scratch_shapes=[pltpu.VMEM((7, tokens, feats), BF16), pltpu.VMEM((2 * tokens, dp * width), BF16),
+                        pltpu.SemaphoreType.DMA((2,))],
         compiler_params=pltpu.CompilerParams(vmem_limit_bytes=8 * MIB),
         cost_estimate=cost(4 * tokens * feats * dp * width, 4 * tokens * dp * width),
         name="join",
-    )(state, sums, message, third, even, odd, *pieces)
+    )(state, sums, message, third, odd, even, embed)
 
 
 def solution(mesh):

time: 17 us -> 16.9 us (level)
  waiting for transfers between devices: 2.52 us -> 0.21 us
  Pallas kernels: 7.64 us -> 9.81 us
    ppermute x5, waiting for transfers between devices: 2.52 us -> 0.21 us  [exchange(): return lax.ppermute(value, axis, [(i, i ^ offset) for i in range(count)])]
    pallas_call x2, Pallas kernels: 1.08 us -> 3.19 us  [the longest x1 2.19 us: local(): pl.pallas_call(functools.partial(final_kernel, dp), out_shape=[pltpu.VMEM...]
  transfers between devices with their start and end apart: 6 -> 6, of which waited for: 1 -> 1; matrix products, arithmetic and copies ran while one was open for 0% -> 0% of each run, Pallas kernels for 39% -> 52%
where the time goes in v5:
time: 16.9 us; the launch traced here: 16.8 us
  Pallas kernels  9.81 us (58%)
  starting transfers between devices  6.74 us (40%)
  waiting for transfers between devices  0.21 us (1%)
    ppermute x5, starting transfers between devices, exchange(): return lax.ppermute(value, axis, [(i, i ^ offset) for i in range(count)])  6.32 us
    pallas_call x1, Pallas kernels, begin(): pl.pallas_call(begin_kernel, out_shape=[pltpu.SMEM((8,), jnp.int32), pltp...  4.23 us
    pallas_call x1, Pallas kernels, local(): pl.pallas_call(functools.partial(middle_kernel, offsets), out_shape=[jax....  2.39 us
    pallas_call x1, Pallas kernels, local(): pl.pallas_call(functools.partial(final_kernel, dp), out_shape=[pltpu.VMEM...  2.19 us
    pallas_call x1, Pallas kernels, local(): pl.pallas_call(join_kernel, out_shape=jax.ShapeDtypeStruct((1, 2 * tokens...  0.99 us
    ppermute x1, starting transfers between devices, swap_odd_pairs(): return lax.ppermute(value, ('dp', 'seq'), pairs)  0.42 us
  transfers between devices with their start and end apart: 6, of which 1 were waited for; matrix products, arithmetic and copies ran while one was open for 0% of the time, Pallas kernels for 52%

profile of v5, /device:TPU:0, one launch (start us, length us, event | category | flops | bytes accessed | tf_op | source)
XLA Modules:
  0.0 16.8 jit_solution(13333279747445152086)
XLA Ops:
  0.0 3.0 %collective-permute-start = (s32[1,3]{1,0:T(1,128)}, s32[1,3]{1,0:T(1,128)S(1)}, u32[]{:S(2)}, u32[]{:S(2)}) collective-permute-start(s32[1,3]{1,0:T(1,128)} %kind_hbm.1), channel_id=1, source_target_pairs={{0,2},{1,3},{2,0},{3,1},{4,6},{5,7},{6,4},{7,5},{8,10},{9,11},{10,... | collective-permute-start | bytes 44 | tf_op jit(solution)/shard_map/ppermute | solution.py:404
  3.0 4.2 %begin.1 = (s32[8]{0:T(128)S(4)}, bf16[3,256,512]{2,1,0:T(8,128)(2,1)S(1)}, bf16[4608,512]{1,0:T(8,128)(2,1)S(1)}, bf16[64,256]{1,0:T(8,128)(2,1)S(1)}, bf16[80,...) custom-call(s32[1,3]{1,0:T(1,128)} %kind_hbm.1, ...), custom_call_target="tpu_custom_call" | custom-call | flops 1245708288 | bytes 4718592 | tf_op jit(solution)/shard_map/begin/pallas_call | solution.py:437
  7.3 0.1 collective-permute-start.1
  7.3 1.6 %collective-permute-start.2 = (bf16[80,288]{1,0:T(8,128)(2,1)S(1)}, bf16[80,288]{1,0:T(8,128)(2,1)S(1)}, u32[]{:S(2)}, u32[]{:S(2)}) collective-permute-start(bf16[80,288]{1,0:T(8,128)(2,1)S(1)} %get-tuple-element.40.rest_0_), channel_id=1, source_target_pairs={{0,16},{8,24},{16,0},{24,8},{1,17},{9,25},{17,1},{25,9},{2,18},{10... | collective-permute-start | bytes 138248 | tf_op jit(solution)/shard_map/ppermute | solution.py:404
  8.9 0.3 %collective-permute-start.3 = (bf16[80,288]{1,0:T(8,128)(2,1)S(1)}, bf16[80,288]{1,0:T(8,128)(2,1)S(1)}, u32[]{:S(2)}, u32[]{:S(2)}) collective-permute-start(bf16[80,288]{1,0:T(8,128)(2,1)S(1)} %get-tuple-element.40.rest_0_), channel_id=1, source_target_pairs={{0,24},{8,16},{16,8},{24,0},{1,25},{9,17},{17,9},{25,1},{2,26},{10... | collective-permute-start | bytes 138248 | tf_op jit(solution)/shard_map/ppermute | solution.py:404
  9.2 0.0 collective-permute-done.rest_7_
  9.2 2.4 %middle.1 = (bf16[80,128]{1,0:T(8,128)(2,1)S(1)}, s32[1]{0:T(128)S(4)}) custom-call(s32[8]{0:T(128)S(4)} %get-tuple-element.24.state_ref, bf16[3,256,512]{2,1,0:T(8,128)(2,1)S(1)} %get-tuple-element.25.x_ref, bf16[4608,512]{1,0:T(8,128)(2,1)S(1)} %get-tuple-element.26.w_ref, bf16[64,256]{1,0:T(8,128)(2,1)S(1)} %get-tuple-element.27.perm_ref, ...), custom_call_target="tpu_custom_call" | custom-call | flops 1245708288 | bytes 4718592 | tf_op jit(solution)/shard_map/middle/pallas_call | solution.py:482
  11.6 0.4 %collective-permute-start.4 = (bf16[80,128]{1,0:T(8,128)(2,1)S(1)}, bf16[80,128]{1,0:T(8,128)(2,1)S(1)}, u32[]{:S(2)}, u32[]{:S(2)}) collective-permute-start(bf16[80,128]{1,0:T(8,128)(2,1)S(1)} %get-tuple-element.39.own_ref), channel_id=1, source_target_pairs={{0,8},{7,15},{1,2},{2,1},{3,4},{4,3},{5,6},{6,5},{8,0},{15,7},{9,1... | collective-permute-start | bytes 61448 | tf_op jit(solution)/shard_map/ppermute | solution.py:414
  12.0 1.4 %collective-permute-start.5 = (bf16[80,128]{1,0:T(8,128)(2,1)S(1)}, bf16[80,128]{1,0:T(8,128)(2,1)S(1)}, u32[]{:S(2)}, u32[]{:S(2)}) collective-permute-start(bf16[80,128]{1,0:T(8,128)(2,1)S(1)} %get-tuple-element.39.own_ref), channel_id=1, source_target_pairs={{0,1},{1,0},{2,3},{3,2},{4,5},{5,4},{6,7},{7,6},{8,9},{9,8},{10,11... | collective-permute-start | bytes 61448 | tf_op jit(solution)/shard_map/ppermute | solution.py:404
  13.4 0.0 collective-permute-done.1.rest_1_
  13.4 0.0 collective-permute-done.2.rest_2_
  13.4 0.0 collective-permute-done.3.rest_3_
  13.4 2.2 %final.1 = (bf16[64,64]{1,0:T(8,128)(2,1)S(1)}, bf16[80,1152]{1,0:T(8,128)(2,1)S(1)}) custom-call(s32[8]{0:T(128)S(4)} %get-tuple-element.24.state_ref, bf16[3,256,512]{2,1,0:T(8,128)(2,1)S(1)} %get-tuple-element.25.x_ref, bf16[4608,512]{1,0:T(8,128)(2,1)S(1)} %get-tuple-element.26.w_ref, bf16[64,256]{1,0:T(8,128)(2,1)S(1)} %get-tuple-element.27.perm_ref, ...), custom_call_target="tpu_custom_call" | custom-call | flops 1245708288 | bytes 4718592 | tf_op jit(solution)/shard_map/final/pallas_call | solution.py:496
  15.6 0.0 collective-permute-done.4.odd_ref
  15.6 0.2 %collective-permute-done.5.even_ref = bf16[80,128]{1,0:T(8,128)(2,1)S(1)} collective-permute-done((bf16[80,128]{1,0:T(8,128)(2,1)S(1)}, bf16[80,128]{1,0:T(8,128)(2,1)S(1)}, u32[]{:S(2)}, u32[]{:S(2)}) %collective-permute-start.5) | collective-permute-done | bytes 20512 | tf_op jit(solution)/shard_map/ppermute | solution.py:404
  15.8 1.0 %join.1 = bf16[1,128,1152]{2,1,0:T(8,128)(2,1)} custom-call(s32[8]{0:T(128)S(4)} %get-tuple-element.24.state_ref, s32[1]{0:T(128)S(4)} %get-tuple-element.38.sums_ref, bf16[80,128]{1,0:T(8,128)(2,1)S(1)} %get-tuple-element.39.own_ref, bf16[64,64]{1,0:T(8,128)(2,1)S(1)} %get-tuple-element.41.third_ref, bf16[80,128]{1,0:T(8,128)(2,1)S(1)} %collective-permute-done.4.odd_ref, ...), custom_call_target="tpu_custom_call" | custom-call | flops 18874368 | bytes 294912 | tf_op jit(solution)/shard_map/join/pallas_call | solution.py:506
Async XLA Ops:
  0.0 9.2 %collective-permute-start = (s32[1,3]{1,0:T(1,128)}, s32[1,3]{1,0:T(1,128)S(1)}, u32[]{:S(2)}, u32[]{:S(2)}) collective-permute-start(s32[1,3]{1,0:T(1,128)} %kind_hbm.1), channel_id=1, source_target_pairs={{0,2},{1,3},{2,0},{3,1},{4,6},{5,7},{6,4},{7,5},{8,10},{9,11},{10,... | collective-permute-start | bytes 44 | tf_op jit(solution)/shard_map/ppermute | solution.py:404
  7.3 6.1 %collective-permute-start.1 = (bf16[80,288]{1,0:T(8,128)(2,1)S(1)}, bf16[80,288]{1,0:T(8,128)(2,1)S(1)}, u32[]{:S(2)}, u32[]{:S(2)}) collective-permute-start(bf16[80,288]{1,0:T(8,128)(2,1)S(1)} %get-tuple-element.40.rest_0_), channel_id=1, source_target_pairs={{0,8},{8,0},{16,24},{24,16},{1,9},{9,1},{17,25},{25,17},{2,10},{10... | collective-permute-start | bytes 138248 | tf_op jit(solution)/shard_map/ppermute | solution.py:404
  7.3 6.0 %collective-permute-start.2 = (bf16[80,288]{1,0:T(8,128)(2,1)S(1)}, bf16[80,288]{1,0:T(8,128)(2,1)S(1)}, u32[]{:S(2)}, u32[]{:S(2)}) collective-permute-start(bf16[80,288]{1,0:T(8,128)(2,1)S(1)} %get-tuple-element.40.rest_0_), channel_id=1, source_target_pairs={{0,16},{8,24},{16,0},{24,8},{1,17},{9,25},{17,1},{25,9},{2,18},{10... | collective-permute-start | bytes 138248 | tf_op jit(solution)/shard_map/ppermute | solution.py:404
  8.9 4.5 %collective-permute-start.3 = (bf16[80,288]{1,0:T(8,128)(2,1)S(1)}, bf16[80,288]{1,0:T(8,128)(2,1)S(1)}, u32[]{:S(2)}, u32[]{:S(2)}) collective-permute-start(bf16[80,288]{1,0:T(8,128)(2,1)S(1)} %get-tuple-element.40.rest_0_), channel_id=1, source_target_pairs={{0,24},{8,16},{16,8},{24,0},{1,25},{9,17},{17,9},{25,1},{2,26},{10... | collective-permute-start | bytes 138248 | tf_op jit(solution)/shard_map/ppermute | solution.py:404
  11.6 4.0 %collective-permute-start.4 = (bf16[80,128]{1,0:T(8,128)(2,1)S(1)}, bf16[80,128]{1,0:T(8,128)(2,1)S(1)}, u32[]{:S(2)}, u32[]{:S(2)}) collective-permute-start(bf16[80,128]{1,0:T(8,128)(2,1)S(1)} %get-tuple-element.39.own_ref), channel_id=1, source_target_pairs={{0,8},{7,15},{1,2},{2,1},{3,4},{4,3},{5,6},{6,5},{8,0},{15,7},{9,1... | collective-permute-start | bytes 61448 | tf_op jit(solution)/shard_map/ppermute | solution.py:414
  12.0 3.8 %collective-permute-start.5 = (bf16[80,128]{1,0:T(8,128)(2,1)S(1)}, bf16[80,128]{1,0:T(8,128)(2,1)S(1)}, u32[]{:S(2)}, u32[]{:S(2)}) collective-permute-start(bf16[80,128]{1,0:T(8,128)(2,1)S(1)} %get-tuple-element.39.own_ref), channel_id=1, source_target_pairs={{0,1},{1,0},{2,3},{3,2},{4,5},{5,4},{6,7},{7,6},{8,9},{9,8},{10,11... | collective-permute-start | bytes 61448 | tf_op jit(solution)/shard_map/ppermute | solution.py:404
